TPU v7x, 512 devices: a whole 4x8x8 slice. The times are simulated.
512 devices in a mesh: dp: 16 (over z, core), ctx: 8 (over y), mp: 4 (over x).
Axes of the slice: x: 4, y: 8, z: 8, core: 2. Of those that a mesh axis runs over, the one named last changes fastest.
Arguments:
- key_cache: bfloat16 [64, 2048, 1024], P('dp', 'ctx', 'mp'), may hold values from -5 to 5
- value_cache: bfloat16 [64, 2048, 1024], P('dp', 'ctx', 'mp'), may hold values from -5 to 5
- lengths: int32 [64], P('dp'), may hold values from 1 to 2048, as said below
- queries: bfloat16 [3, 64, 8192], P(None, 'dp', 'mp'), may hold values from -64 to 64
- fresh_pairs: bfloat16 [3, 2, 64, 1024], P(None, None, 'dp', 'mp'), may hold values from -5 to 5
- recent_inputs: bfloat16 [64, 3, 16384], P('dp', None, ('ctx', 'mp')), may hold values from -5 to 5
- scan_state: float32 [64, 16, 16384], P('dp', None, ('ctx', 'mp')), may hold values from -5 to 5
- mamba_inputs: bfloat16 [3, 2, 64, 16384], P(None, None, 'dp', ('ctx', 'mp')), may hold values from -5 to 5
- step_sizes: float32 [3, 64, 16384], P(None, 'dp', ('ctx', 'mp')), may hold values from 0.001 to 0.2
- filter_taps: bfloat16 [4, 16384], P(None, ('ctx', 'mp')), may hold values from -3 to 3
- filter_bias: float32 [16384], P(('ctx', 'mp')), may hold values from -3 to 3
- decay_logs: float32 [16, 16384], P(None, ('ctx', 'mp')), may hold values from 0 to 2.77
- skip_gain: float32 [16384], P(('ctx', 'mp')), may hold values from 0.5 to 1.5
- select_weight: bfloat16 [32, 16384], P(None, ('ctx', 'mp')), may hold values from -0.046875 to 0.046875
- target_group: int32 [64], P('dp'), may hold values from 0 to 15, as said below
- target_slot: int32 [64], P('dp'), may hold values from 0 to 3
Outputs:
- attended: bfloat16 [3, 64, 8192], P(None, 'dp', 'mp')
- mamba_output: bfloat16 [3, 64, 16384], P(None, 'dp', ('ctx', 'mp'))
Inputs may be any that keep to these rules, and one draw needn't show every extreme that they name: The pairs (target_group, target_slot) name every slot of every group exactly once, and the 4 requests of one group go to 4 different groups. `lengths`: at least one request uses all 2048 positions.
All inputs are finite; a program needn't handle non-finite values.
Results may differ from a plain program's by a relative error of at most 0.0051.
Values may be sent and summed in bfloat16 or wider, within the bound.
A program may use at most 64 MiB of HBM per device.

v0:
```python
import jax
import jax.numpy as jnp
from jax import lax
from jax.sharding import PartitionSpec as P

HEADS = 64
KV_HEADS = 8
HEAD = 128


NEGATIVE = -1e30


def merged_2(value, axis, join):
    pieces = jax.tree.map(lambda part: lax.all_gather(part, axis), value)
    head = jax.tree.map(lambda part: part[0], pieces)
    tail = jax.tree.map(lambda part: part[1:], pieces)
    running, _ = lax.scan(lambda running, slab: (join(running, slab), None), head, tail)
    return running


def local_stats(question, key_rows, value_rows, usable, shared_heads):
    slot_count = question.shape[0]
    group_share = HEADS // KV_HEADS
    asked_rows = question.reshape(slot_count, shared_heads, group_share, HEAD)
    keyed = key_rows.reshape(slot_count, -1, shared_heads, HEAD)
    valued = value_rows.reshape(slot_count, -1, shared_heads, HEAD)
    scores = jnp.einsum(
        "sgqd,spgd->sgqp", asked_rows, keyed, preferred_element_type=jnp.float32
    ) * HEAD ** (-0.5)
    allowed = usable[:, None, None, :]
    scores = jnp.where(allowed, scores, NEGATIVE)
    highest = jnp.max(scores, axis=-1)
    weights = jnp.where(allowed, jnp.exp(scores - highest[..., None]), 0.0)
    weight_sum = jnp.sum(weights, axis=-1)
    weighted = jnp.einsum(
        "sgqp,spgd->sgqd", weights.astype(jnp.bfloat16), valued, preferred_element_type=jnp.float32
    )
    return (highest, weight_sum, weighted)


def joined(earlier, second):
    highest = jnp.maximum(earlier[0], second[0])
    former = jnp.exp(earlier[0] - highest)
    latter = jnp.exp(second[0] - highest)
    return (
        highest,
        earlier[1] * former + second[1] * latter,
        earlier[2] * former[..., None] + second[2] * latter[..., None],
    )


def across_blocks(stats):
    return merged_2(stats, "ctx", joined)


def finish(question, merged, recent_keys, recent_values, shared_heads):
    highest, weight_sum, weighted = merged
    slot_count = question.shape[0]
    group_share = HEADS // KV_HEADS
    asked_rows = question.reshape(slot_count, shared_heads, group_share, HEAD)
    fresh_keys = recent_keys.reshape(slot_count, recent_keys.shape[1], shared_heads, HEAD)
    fresh_values = recent_values.reshape(
        slot_count, recent_values.shape[1], shared_heads, HEAD
    ).astype(jnp.float32)
    recent_scores = jnp.einsum(
        "sgqd,sngd->sgqn", asked_rows, fresh_keys, preferred_element_type=jnp.float32
    ) * HEAD ** (-0.5)
    overall = jnp.maximum(highest, jnp.max(recent_scores, axis=-1))
    retain = jnp.exp(highest - overall)
    recent_weights = jnp.exp(recent_scores - overall[..., None])
    numerator = weighted * retain[..., None] + jnp.einsum(
        "sgqn,sngd->sgqd", recent_weights, fresh_values, precision=lax.Precision.HIGHEST
    )
    denominator = weight_sum * retain + jnp.sum(recent_weights, axis=-1)
    return (numerator / denominator[..., None]).reshape(slot_count, -1).astype(jnp.bfloat16)


def mamba_step(
    recent_rows,
    hidden_state,
    fresh_input,
    gate_input,
    step_rows,
    filter_taps,
    filter_bias,
    decay_logs,
    skip_gain,
    select_weight,
):
    window = jnp.concatenate([recent_rows, fresh_input[:, None, :]], axis=1)
    filtered = (
        jnp.sum(window.astype(jnp.float32) * filter_taps.astype(jnp.float32)[None], axis=1)
        + filter_bias
    )
    filtered = lax.optimization_barrier((filtered * jax.nn.sigmoid(filtered)).astype(jnp.bfloat16))
    partial_sums = jnp.einsum(
        "ri,si->rs", filtered, select_weight, preferred_element_type=jnp.float32
    )
    selection = lax.psum(partial_sums, ("ctx", "mp"))
    state_width = selection.shape[1] // 2
    input_select = selection[:, :state_width]
    output_select = selection[:, state_width:]
    as_float = filtered.astype(jnp.float32)
    decays = jnp.exp(-step_rows[:, None, :] * jnp.exp(decay_logs)[None])
    new_state = (
        decays * hidden_state
        + step_rows[:, None, :] * input_select[:, :, None] * as_float[:, None, :]
    )
    readout = jnp.sum(output_select[:, :, None] * new_state, axis=1) + skip_gain * as_float
    result = (readout * jax.nn.silu(gate_input.astype(jnp.float32))).astype(jnp.bfloat16)
    return (window[:, 1:], new_state, result)


def pack_rows(source_rows, row_index, present):
    picked = jnp.take(source_rows, row_index, axis=0)
    shaped = (present.shape[0],) + (1,) * (source_rows.ndim - 1)
    return jnp.where(present.reshape(shaped), picked, jnp.zeros((), source_rows.dtype))


def on_device(
    key_cache,
    value_cache,
    lengths,
    queries,
    fresh_pairs,
    recent_inputs,
    scan_state,
    mamba_inputs,
    step_sizes,
    filter_taps,
    filter_bias,
    decay_logs,
    skip_gain,
    select_weight,
    target_group,
    target_slot,
):
    shared_heads = KV_HEADS // lax.axis_size("mp")
    group_count = lax.axis_size("dp")
    slot_count = key_cache.shape[0]
    block_size = key_cache.shape[1]
    positions = lax.axis_index("ctx") * block_size + jnp.arange(block_size, dtype=jnp.int32)
    usable = positions[None, :] < lengths[:, None]
    opening = across_blocks(local_stats(queries[0], key_cache, value_cache, usable, shared_heads))
    attended = [
        finish(
            queries[0],
            opening,
            fresh_pairs[0, 0][:, None],
            fresh_pairs[0, 1][:, None],
            shared_heads,
        )
    ]
    carried, hidden_state, result = mamba_step(
        recent_inputs,
        scan_state,
        mamba_inputs[0, 0],
        mamba_inputs[0, 1],
        step_sizes[0],
        filter_taps,
        filter_bias,
        decay_logs,
        skip_gain,
        select_weight,
    )
    mixed_out = [result]
    peer_ids = jnp.arange(group_count, dtype=jnp.int32)
    slot_ids = jnp.arange(slot_count, dtype=jnp.int32)
    outgoing = target_group[None, :] == peer_ids[:, None]
    has_outgoing = jnp.any(outgoing, axis=1)
    out_index = jnp.sum(jnp.where(outgoing, slot_ids[None, :], 0), axis=1)
    landing = jnp.where(has_outgoing, jnp.take(target_slot, out_index), -1).astype(jnp.float32)
    state_rows, carried_rows, pair_rows, length_rows, landing_rows = (
        lax.all_to_all(
            pack_rows(hidden_state, out_index, has_outgoing),
            "dp",
            split_axis=0,
            concat_axis=0,
            tiled=True,
        ),
        lax.all_to_all(
            pack_rows(carried.astype(jnp.float32), out_index, has_outgoing),
            "dp",
            split_axis=0,
            concat_axis=0,
            tiled=True,
        ),
        lax.all_to_all(
            pack_rows(
                jnp.swapaxes(fresh_pairs[0], 0, 1).astype(jnp.float32), out_index, has_outgoing
            ),
            "dp",
            split_axis=0,
            concat_axis=0,
            tiled=True,
        ),
        lax.all_to_all(
            pack_rows(lengths.astype(jnp.float32), out_index, has_outgoing),
            "dp",
            split_axis=0,
            concat_axis=0,
            tiled=True,
        ),
        lax.all_to_all(landing, "dp", split_axis=0, concat_axis=0, tiled=True),
    )
    arriving = landing_rows.astype(jnp.int32)[None, :] == slot_ids[:, None]
    anchor = jnp.sum(jnp.where(arriving, peer_ids[None, :], 0), axis=1)
    hidden_state = jnp.take(state_rows, anchor, axis=0)
    carried = jnp.take(carried_rows, anchor, axis=0).astype(jnp.bfloat16)
    moved_pairs = jnp.take(pair_rows, anchor, axis=0).astype(jnp.bfloat16)
    moved_keys, moved_values = (
        lax.all_to_all(
            pack_rows(key_cache, out_index, has_outgoing),
            "dp",
            split_axis=0,
            concat_axis=0,
            tiled=True,
        ),
        lax.all_to_all(
            pack_rows(value_cache, out_index, has_outgoing),
            "dp",
            split_axis=0,
            concat_axis=0,
            tiled=True,
        ),
    )
    cache_keys = jnp.take(moved_keys, anchor, axis=0)
    cache_values = jnp.take(moved_values, anchor, axis=0)
    moved_lengths = jnp.take(length_rows, anchor, axis=0).astype(jnp.int32)
    moved_usable = positions[None, :] < moved_lengths[:, None]
    recent_keys = moved_pairs[:, 0][:, None]
    recent_values = moved_pairs[:, 1][:, None]
    for number in (1, 2):
        question = queries[number]
        recent_keys = jnp.concatenate([recent_keys, fresh_pairs[number, 0][:, None]], axis=1)
        recent_values = jnp.concatenate([recent_values, fresh_pairs[number, 1][:, None]], axis=1)
        attended.append(
            finish(
                question,
                across_blocks(
                    local_stats(question, cache_keys, cache_values, moved_usable, shared_heads)
                ),
                recent_keys,
                recent_values,
                shared_heads,
            )
        )
        carried, hidden_state, result = mamba_step(
            carried,
            hidden_state,
            mamba_inputs[number, 0],
            mamba_inputs[number, 1],
            step_sizes[number],
            filter_taps,
            filter_bias,
            decay_logs,
            skip_gain,
            select_weight,
        )
        mixed_out.append(result)
    return (jnp.stack(attended), jnp.stack(mixed_out))


def solution(mesh):
    placed = (
        P("dp", "ctx", "mp"),
        P("dp", "ctx", "mp"),
        P("dp"),
        P(None, "dp", "mp"),
        P(None, None, "dp", "mp"),
        P("dp", None, ("ctx", "mp")),
        P("dp", None, ("ctx", "mp")),
        P(None, None, "dp", ("ctx", "mp")),
        P(None, "dp", ("ctx", "mp")),
        P(None, ("ctx", "mp")),
        P(("ctx", "mp")),
        P(None, ("ctx", "mp")),
        P(("ctx", "mp")),
        P(None, ("ctx", "mp")),
        P("dp"),
        P("dp"),
    )
    return jax.shard_map(
        on_device,
        mesh=mesh,
        in_specs=placed,
        out_specs=(P(None, "dp", "mp"), P(None, "dp", ("ctx", "mp"))),
        check_vma=False,
    )
```

profile of v0, /device:TPU:16, one launch (start us, length us, event | category | flops | bytes accessed | tf_op | source)
XLA Modules:
  0.0 445.2 jit_solution(18231715045159581664)
XLA Ops:
  4.2 10.4 %all-to-all-start = ((f32[16,1,1]{2,1,0:T(1,128)}), f32[16,1,1]{2,1,0:T(1,128)S(1)}, u32[]{:S(2)}, u32[]{:S(2)}) async-start(f32[16,1,1]{2,1,0:T(1,128)} %copy.119), calls=%async_computation | async-start | bytes 16384 | tf_op jit(solution)/shard_map/all_to_all | solution.py:205
  24.5 7.2 %all-to-all-start.1 = ((f32[16,1,1]{2,1,0:T(1,128)}), f32[16,1,1]{2,1,0:T(1,128)S(1)}, u32[]{:S(2)}, u32[]{:S(2)}) async-start(f32[16,1,1]{2,1,0:T(1,128)} %copy.120), calls=%async_computation.1 | async-start | bytes 16384 | tf_op jit(solution)/shard_map/all_to_all | solution.py:198
  32.3 7.0 %all-to-all-done.1 = f32[16,1,1]{2,1,0:T(1,128)S(1)} async-done(((f32[16,1,1]{2,1,0:T(1,128)}), f32[16,1,1]{2,1,0:T(1,128)S(1)}, u32[]{:S(2)}, u32[]{:S(2)}) %all-to-all-start.1) | async-done | bytes 96 | tf_op jit(solution)/shard_map/all_to_all | solution.py:198
  39.3 3.5 all-to-all-start.5
  43.6 6.9 %all-to-all-done.5 = bf16[16,3,512]{2,1,0:T(4,128)(2,1)S(1)} async-done(((bf16[16,3,512]{2,1,0:T(4,128)(2,1)}), bf16[16,3,512]{2,1,0:T(4,128)(2,1)S(1)}, u32[]{:S(2)}, u32[]{:S(2)}) %all-to-all-start.5) | async-done | bytes 49184 | tf_op jit(solution)/shard_map/all_to_all | solution.py:182
  50.6 3.5 all-to-all-start.4
  55.3 64.0 %all-reduce = (f32[4,32]{1,0:T(4,128)S(1)}, f32[4,32]{1,0:T(4,128)S(1)}, f32[4,32]{1,0:T(4,128)S(1)}) all-reduce(f32[4,32]{1,0:T(4,128)S(1)} %fusion.137, f32[4,32]{1,0:T(4,128)S(1)} %fusion.138, f32[4,32]{1,0:T(4,128)S(1)} %fusion.139), channel_id=1, replica_groups=mesh['dp'=16,'ctx'=8,'mp'=4] {'ctx','mp'}, use_global_device_ids=true, to_apply=%region_20.23 | all-reduce | flops 384 | bytes 3072 | tf_op jit(solution)/shard_map/psum | solution.py:100
  121.1 7.1 %all-to-all-start.6 = ((f32[16,16,512]{2,1,0:T(8,128)}), f32[16,16,512]{2,1,0:T(8,128)}, u32[]{:S(2)}, u32[]{:S(2)}) async-start(f32[16,16,512]{2,1,0:T(8,128)} %select_select_fusion.2), calls=%async_computation.6 | async-start | bytes 1048576 | tf_op jit(solution)/shard_map/all_to_all | solution.py:175
  128.9 2.0 gather_fusion.9
  130.9 4.1 select_select_fusion
  135.0 9.3 %all-to-all-done.6 = f32[16,16,512]{2,1,0:T(8,128)} async-done(((f32[16,16,512]{2,1,0:T(8,128)}), f32[16,16,512]{2,1,0:T(8,128)}, u32[]{:S(2)}, u32[]{:S(2)}) %all-to-all-start.6) | async-done | bytes 524320 | tf_op jit(solution)/shard_map/all_to_all | solution.py:175
  144.3 4.3 all-to-all-start.3
  149.3 34.9 %all-gather = f32[32,2,8]{2,1,0:T(2,128)S(1)} all-gather(f32[4,2,8]{2,1,0:T(2,128)S(1)} %get-tuple-element.251), channel_id=2, replica_groups=mesh['dp'=16,'ctx'=8,'mp'=4] {'ctx'}, dimensions={0}, use_global_device_ids=true | all-gather | bytes 2304 | tf_op jit(solution)/shard_map/all_gather | solution.py:15
  184.4 24.5 %all-gather.1 = f32[32,2,8]{2,1,0:T(2,128)S(1)} all-gather(f32[4,2,8]{2,1,0:T(2,128)S(1)} %fusion.36), channel_id=3, replica_groups=mesh['dp'=16,'ctx'=8,'mp'=4] {'ctx'}, dimensions={0}, use_global_device_ids=true | all-gather | bytes 2304 | tf_op jit(solution)/shard_map/all_gather | solution.py:15
  209.1 24.8 %all-gather.2 = f32[32,2,8,128]{3,2,1,0:T(8,128)S(1)} all-gather(f32[4,2,8,128]{3,2,1,0:T(8,128)S(1)} %fusion.26), channel_id=4, replica_groups=mesh['dp'=16,'ctx'=8,'mp'=4] {'ctx'}, dimensions={0}, use_global_device_ids=true | all-gather | bytes 294912 | tf_op jit(solution)/shard_map/all_gather | solution.py:15
  234.0 7.5 %all-to-all-start.2 = ((bf16[16,256,256]{2,1,0:T(8,128)(2,1)}), bf16[16,256,256]{2,1,0:T(8,128)(2,1)}, u32[]{:S(2)}, u32[]{:S(2)}) async-start(bf16[16,256,256]{2,1,0:T(8,128)(2,1)} %get-tuple-element.240), calls=%async_computation.2 | async-start | bytes 4194304 | tf_op jit(solution)/shard_map/all_to_all | solution.py:213
  246.8 43.9 %all-to-all-done.2 = bf16[16,256,256]{2,1,0:T(8,128)(2,1)} async-done(((bf16[16,256,256]{2,1,0:T(8,128)(2,1)}), bf16[16,256,256]{2,1,0:T(8,128)(2,1)}, u32[]{:S(2)}, u32[]{:S(2)}) %all-to-all-start.2) | async-done | bytes 2097184 | tf_op jit(solution)/shard_map/all_to_all | solution.py:213
  290.7 2.2 gather_fusion.10
  293.7 24.5 %all-gather.6 = f32[32,2,8]{2,1,0:T(2,128)S(1)} all-gather(f32[4,2,8]{2,1,0:T(2,128)S(1)} %get-tuple-element.243), channel_id=8, replica_groups=mesh['dp'=16,'ctx'=8,'mp'=4] {'ctx'}, dimensions={0}, use_global_device_ids=true | all-gather | bytes 2304 | tf_op jit(solution)/shard_map/all_gather | solution.py:15
  318.4 24.5 %all-gather.7 = f32[32,2,8]{2,1,0:T(2,128)S(1)} all-gather(f32[4,2,8]{2,1,0:T(2,128)S(1)} %get-tuple-element.136), channel_id=9, replica_groups=mesh['dp'=16,'ctx'=8,'mp'=4] {'ctx'}, dimensions={0}, use_global_device_ids=true | all-gather | bytes 2304 | tf_op jit(solution)/shard_map/all_gather | solution.py:15
  343.1 24.8 %all-gather.8 = f32[32,2,8,128]{3,2,1,0:T(8,128)S(1)} all-gather(f32[4,2,8,128]{3,2,1,0:T(8,128)S(1)} %fusion.20), channel_id=10, replica_groups=mesh['dp'=16,'ctx'=8,'mp'=4] {'ctx'}, dimensions={0}, use_global_device_ids=true | all-gather | bytes 294912 | tf_op jit(solution)/shard_map/all_gather | solution.py:15
  367.9 24.5 %all-gather.3 = f32[32,2,8]{2,1,0:T(2,128)S(1)} all-gather(f32[4,2,8]{2,1,0:T(2,128)S(1)} %get-tuple-element.245), channel_id=5, replica_groups=mesh['dp'=16,'ctx'=8,'mp'=4] {'ctx'}, dimensions={0}, use_global_device_ids=true | all-gather | bytes 2304 | tf_op jit(solution)/shard_map/all_gather | solution.py:15
  392.6 24.5 %all-gather.4 = f32[32,2,8]{2,1,0:T(2,128)S(1)} all-gather(f32[4,2,8]{2,1,0:T(2,128)S(1)} %get-tuple-element.135), channel_id=6, replica_groups=mesh['dp'=16,'ctx'=8,'mp'=4] {'ctx'}, dimensions={0}, use_global_device_ids=true | all-gather | bytes 2304 | tf_op jit(solution)/shard_map/all_gather | solution.py:15
  417.1 24.8 %all-gather.5 = f32[32,2,8,128]{3,2,1,0:T(8,128)S(1)} all-gather(f32[4,2,8,128]{3,2,1,0:T(8,128)S(1)} %fusion.22), channel_id=7, replica_groups=mesh['dp'=16,'ctx'=8,'mp'=4] {'ctx'}, dimensions={0}, use_global_device_ids=true | all-gather | bytes 294912 | tf_op jit(solution)/shard_map/all_gather | solution.py:15
  (189 shorter events, 31.8 us)
Async XLA Ops:
  0.6 128.3 %copy-start = (bf16[4,256,256]{2,1,0:T(8,128)(2,1)S(1)}, bf16[4,256,256]{2,1,0:T(8,128)(2,1)}, u32[]{:S(2)}) copy-start(bf16[4,256,256]{2,1,0:T(8,128)(2,1)} %param.26) | copy-start | bytes 1572868
  0.6 54.2 %copy-start.7 = (f32[512]{0:T(512)S(1)}, f32[512]{0:T(512)}, u32[]{:S(2)}) copy-start(f32[512]{0:T(512)} %param.36) | copy-start | bytes 6148
  0.7 54.3 %copy-start.2 = (bf16[32,512]{1,0:T(8,128)(2,1)S(1)}, bf16[32,512]{1,0:T(8,128)(2,1)}, u32[]{:S(2)}) copy-start(bf16[32,512]{1,0:T(8,128)(2,1)} %param.39) | copy-start | bytes 98308
  0.7 118.7 %copy-start.3 = (f32[4,16,512]{2,1,0:T(8,128)S(1)}, f32[4,16,512]{2,1,0:T(8,128)}, u32[]{:S(2)}) copy-start(f32[4,16,512]{2,1,0:T(8,128)} %param.32) | copy-start | bytes 393220
  4.2 20.2 %all-to-all-start = ((f32[16,1,1]{2,1,0:T(1,128)}), f32[16,1,1]{2,1,0:T(1,128)S(1)}, u32[]{:S(2)}, u32[]{:S(2)}) async-start(f32[16,1,1]{2,1,0:T(1,128)} %copy.119), calls=%async_computation | async-start | bytes 16384 | tf_op jit(solution)/shard_map/all_to_all | solution.py:205
  24.5 14.8 %all-to-all-start.1 = ((f32[16,1,1]{2,1,0:T(1,128)}), f32[16,1,1]{2,1,0:T(1,128)S(1)}, u32[]{:S(2)}, u32[]{:S(2)}) async-start(f32[16,1,1]{2,1,0:T(1,128)} %copy.120), calls=%async_computation.1 | async-start | bytes 16384 | tf_op jit(solution)/shard_map/all_to_all | solution.py:198
  39.3 11.3 %all-to-all-start.5 = ((bf16[16,3,512]{2,1,0:T(4,128)(2,1)}), bf16[16,3,512]{2,1,0:T(4,128)(2,1)S(1)}, u32[]{:S(2)}, u32[]{:S(2)}) async-start(bf16[16,3,512]{2,1,0:T(4,128)(2,1)} %select_select_fusion.3), calls=%async_computation.5 | async-start | bytes 131072 | tf_op jit(solution)/shard_map/all_to_all | solution.py:182
  43.6 84.6 %copy-start.1 = (bf16[4,256,256]{2,1,0:T(8,128)(2,1)S(1)}, bf16[4,256,256]{2,1,0:T(8,128)(2,1)}, u32[]{:S(2)}) copy-start(bf16[4,256,256]{2,1,0:T(8,128)(2,1)} %param.27) | copy-start | bytes 1572868
  50.6 70.5 %all-to-all-start.4 = ((bf16[16,2,256]{2,1,0:T(2,128)(2,1)}), bf16[16,2,256]{2,1,0:T(2,128)(2,1)S(1)}, u32[]{:S(2)}, u32[]{:S(2)}) async-start(bf16[16,2,256]{2,1,0:T(2,128)(2,1)} %select_select_fusion.4), calls=%async_computation.4 | async-start | bytes 32768 | tf_op jit(solution)/shard_map/all_to_all | solution.py:189
  121.1 23.2 %all-to-all-start.6 = ((f32[16,16,512]{2,1,0:T(8,128)}), f32[16,16,512]{2,1,0:T(8,128)}, u32[]{:S(2)}, u32[]{:S(2)}) async-start(f32[16,16,512]{2,1,0:T(8,128)} %select_select_fusion.2), calls=%async_computation.6 | async-start | bytes 1048576 | tf_op jit(solution)/shard_map/all_to_all | solution.py:175
  144.3 4.3 copy-start.6
  144.3 4.5 %copy-start.4 = (bf16[3,4,2048]{2,1,0:T(4,128)(2,1)S(1)}, bf16[3,4,2048]{2,1,0:T(4,128)(2,1)}, u32[]{:S(2)}) copy-start(bf16[3,4,2048]{2,1,0:T(4,128)(2,1)} %param.29) | copy-start | bytes 147460
  144.3 4.6 %copy-start.9 = (s32[4]{0:T(128)S(1)}, s32[4]{0:T(128)}, u32[]{:S(2)}) copy-start(s32[4]{0:T(128)} %param.28) | copy-start | bytes 52
  144.3 89.7 %all-to-all-start.3 = ((bf16[16,256,256]{2,1,0:T(8,128)(2,1)}), bf16[16,256,256]{2,1,0:T(8,128)(2,1)S(1)}, u32[]{:S(2)}, u32[]{:S(2)}) async-start(bf16[16,256,256]{2,1,0:T(8,128)(2,1)} %get-tuple-element.239), calls=%async_computation.3 | async-start | bytes 4194304 | tf_op jit(solution)/shard_map/all_to_all | solution.py:220
  234.0 11.5 %copy-start.5 = (bf16[3,2,4,512]{3,2,1,0:T(4,128)(2,1)S(1)}, bf16[3,2,4,512]{3,2,1,0:T(4,128)(2,1)}, u32[]{:S(2)}) copy-start(bf16[3,2,4,512]{3,2,1,0:T(4,128)(2,1)} %param.33) | copy-start | bytes 73732
  234.0 11.5 %copy-start.8 = (f32[512]{0:T(512)S(1)}, f32[512]{0:T(512)}, u32[]{:S(2)}) copy-start(f32[512]{0:T(512)} %param.38) | copy-start | bytes 6148
  234.0 56.7 %all-to-all-start.2 = ((bf16[16,256,256]{2,1,0:T(8,128)(2,1)}), bf16[16,256,256]{2,1,0:T(8,128)(2,1)}, u32[]{:S(2)}, u32[]{:S(2)}) async-start(bf16[16,256,256]{2,1,0:T(8,128)(2,1)} %get-tuple-element.240), calls=%async_computation.2 | async-start | bytes 4194304 | tf_op jit(solution)/shard_map/all_to_all | solution.py:213
where the time goes:
time: 446 us; the launch traced here: 445 us
  blocking collectives  296 us (66%)
  waiting for transfers between devices  67.2 us (15%)
  starting transfers between devices  43.6 us (10%)
  local copies, waits for them, and re-layouts  18 us (4%)
  other arithmetic  16.1 us (4%)
    all_gather x9, blocking collectives, merged_2(): pieces = jax.tree.map(lambda part: lax.all_gather(part, axis), value)  232 us
    psum x1, blocking collectives, mamba_step(): selection = lax.psum(partial_sums, ('ctx', 'mp'))  64 us
    all_to_all x1, waiting for transfers between devices, on_device(): lax.all_to_all(pack_rows(key_cache, out_index, has_outgoing), 'dp', split...  43.9 us
    all_to_all x1, starting transfers between devices, on_device(): lax.all_to_all(landing, 'dp', split_axis=0, concat_axis=0, tiled=True)  10.4 us
    all_to_all x1, waiting for transfers between devices, on_device(): lax.all_to_all(pack_rows(hidden_state, out_index, has_outgoing), 'dp', sp...  9.27 us
  transfers between devices with their start and end apart: 7, of which 4 were waited for; matrix products, arithmetic and copies ran while one was open for 6% of the time, Pallas kernels for 0%

commit v1 on v0

v1 whole, which is shorter than its diff:
```python
import functools

import jax
import jax.numpy as jnp
from jax import lax
from jax.experimental import pallas as pl
from jax.experimental.pallas import tpu as pltpu
from jax.sharding import PartitionSpec as P

HEAD = 128
NEGATIVE = -1e30
SCALE = HEAD**-0.5
MESH = pl.DeviceIdType.MESH
F32 = jnp.float32
BF16 = jnp.bfloat16

N_DP = 16
N_CTX = 8
N_MP = 4
SLOTS = 4
BLOCK = 256
CHAN = 512
CHUNKS = CHAN // 128
STATE = 16

ROW_Q = 0
ROW_F = 32
ROW_M = 40
ROW_S = 56
MSG = 64


def kernel(
    lengths,
    target_group,
    target_slot,
    key_ref,
    value_ref,
    query_ref,
    fresh_ref,
    recent_ref,
    state_ref,
    inputs_ref,
    steps_ref,
    taps_ref,
    bias_ref,
    decay_ref,
    skip_ref,
    select_ref,
    att_ref,
    mam_ref,
    table_out,
    table_in,
    member,
    rows_new,
    rows_old,
    ask_out,
    ask_in,
    moved,
    asked,
    fresh_rows,
    filt,
    sel_out,
    sel_mp,
    sel_sum,
    sel_ctx,
    part_out,
    part_in,
    fin_out,
    fin_in,
    scan_rows,
    mam_rows,
    mam_out,
    mam_in,
    ans_out,
    ans_in,
    back_rows,
    send_sem,
    recv_sem,
):
    d = lax.axis_index("dp")
    c = lax.axis_index("ctx")
    m = lax.axis_index("mp")

    def over_dp(fn):
        def body(k, carry):
            fn(lax.rem(d + k, N_DP))
            return carry

        lax.fori_loop(1, N_DP, body, 0)

    def over_ctx(fn):
        def body(k, carry):
            fn(lax.rem(c + k, N_CTX))
            return carry

        lax.fori_loop(1, N_CTX, body, 0)

    def over_mp(fn):
        def body(k, carry):
            fn(lax.rem(m + k, N_MP))
            return carry

        lax.fori_loop(1, N_MP, body, 0)

    def send(src, dst, phase, device):
        pltpu.make_async_remote_copy(
            src_ref=src,
            dst_ref=dst,
            send_sem=send_sem.at[phase],
            recv_sem=recv_sem.at[phase],
            device_id=device,
            device_id_type=MESH,
        ).start()

    def arrived(buffer, phase, count):
        part = buffer.at[pl.ds(0, count)]
        pltpu.make_async_copy(part, part, recv_sem.at[phase]).wait()

    def sent(buffer, phase, count):
        part = buffer.at[pl.ds(0, count)]
        pltpu.make_async_copy(part, part, send_sem.at[phase]).wait()

    barrier = pltpu.get_barrier_semaphore()
    over_dp(lambda p: pl.semaphore_signal(barrier, inc=1, device_id={"dp": p}, device_id_type=MESH))
    over_ctx(lambda p: pl.semaphore_signal(barrier, inc=1, device_id={"ctx": p}, device_id_type=MESH))
    over_mp(lambda p: pl.semaphore_signal(barrier, inc=1, device_id={"mp": p}, device_id_type=MESH))

    lane = lax.broadcasted_iota(jnp.int32, (1, 128), 1)
    landing = jnp.full((1, 128), -1, jnp.int32)
    for s in range(SLOTS):
        landing = jnp.where(lane == s, target_group[s] * SLOTS + target_slot[s], landing)
    table_out[0] = landing
    table_in[d] = landing
    pl.semaphore_wait(barrier, (N_DP - 1) + (N_CTX - 1) + (N_MP - 1))

    over_dp(lambda p: send(table_out.at[0], table_in.at[d], 0, {"dp": p}))

    for t in (1, 2):
        q = query_ref[t].astype(F32)
        for j in range(16):
            rows_new[pl.ds(ROW_Q + (t - 1) * 16 + j, SLOTS, stride=MSG), :] = q[:, j * 128 : (j + 1) * 128]
        for kv in range(2):
            f = fresh_ref[t, kv].astype(F32)
            for h in range(2):
                rows_new[pl.ds(ROW_F + (t - 1) * 4 + kv * 2 + h, SLOTS, stride=MSG), :] = f[:, h * 128 : (h + 1) * 128]
        for w in range(2):
            x = inputs_ref[t, w].astype(F32)
            for ch in range(CHUNKS):
                rows_new[pl.ds(ROW_M + (t - 1) * 8 + w * 4 + ch, SLOTS, stride=MSG), :] = x[:, ch * 128 : (ch + 1) * 128]
        x = steps_ref[t]
        for ch in range(CHUNKS):
            rows_new[pl.ds(ROW_S + (t - 1) * 4 + ch, SLOTS, stride=MSG), :] = x[:, ch * 128 : (ch + 1) * 128]
    q = query_ref[0].astype(F32)
    for j in range(16):
        rows_old[pl.ds(j, SLOTS, stride=24), :] = q[:, j * 128 : (j + 1) * 128]
    for kv in range(2):
        f = fresh_ref[0, kv].astype(F32)
        for h in range(2):
            rows_old[pl.ds(16 + kv * 2 + h, SLOTS, stride=24), :] = f[:, h * 128 : (h + 1) * 128]

    arrived(table_in, 0, N_DP - 1)
    table = table_in[...].reshape(N_DP, 128)
    for i in range(SLOTS):
        hit = jnp.where(table == d * SLOTS + i, 1.0, 0.0).astype(F32)
        member[i] = jnp.broadcast_to(jnp.max(hit, axis=1, keepdims=True), (N_DP, 128))

    def ask(p):
        total = rows_new[0:MSG, :] * member[0, pl.ds(p, 1), :]
        for i in range(1, SLOTS):
            total += rows_new[i * MSG : (i + 1) * MSG, :] * member[i, pl.ds(p, 1), :]
        return total.astype(BF16)

    def ask_one(p):
        ask_out[p] = ask(p)
        send(ask_out.at[p], ask_in.at[d], 1, {"dp": p})

    over_dp(ask_one)
    ask_in[d] = ask(d)

    taps = taps_ref[...].astype(F32)
    bias = bias_ref[...]
    recent = recent_ref[...].astype(F32)
    window = [recent[:, k, :] for k in range(3)] + [inputs_ref[0, 0].astype(F32)]

    def filtered(parts):
        total = parts[0] * taps[0:1, :]
        for k in range(1, 4):
            total += parts[k] * taps[k : k + 1, :]
        total += bias
        return (total * jax.nn.sigmoid(total)).astype(BF16).astype(F32)

    filt[0, 0:SLOTS, :] = filtered(window)
    rates = jnp.exp(decay_ref[...])

    arrived(ask_in, 1, N_DP - 1)
    for s in range(SLOTS):
        moved[s * MSG : (s + 1) * MSG, :] = ask_in[target_group[s]].astype(F32)

    def moved_rows(row):
        return jnp.concatenate([moved[pl.ds(row + ch, SLOTS, stride=MSG), :] for ch in range(CHUNKS)], axis=1)

    for t in (1, 2):
        window = window[1:] + [moved_rows(ROW_M + (t - 1) * 8)]
        filt[t, 0:SLOTS, :] = filtered(window)
    weight = select_ref[...]
    weight = jnp.concatenate([weight] * SLOTS, axis=0)
    own = lax.broadcasted_iota(jnp.int32, (8, 128), 1) // 32 == lax.broadcasted_iota(jnp.int32, (8, 128), 0)
    picks = []
    for t in range(3):
        product = lax.dot_general(
            filt[t].astype(BF16), weight, (((1,), (1,)), ((), ())), preferred_element_type=F32
        )
        picks.append(jnp.sum(jnp.where(own, product, 0.0), axis=0, keepdims=True))
    sel_out[0] = jnp.concatenate(picks + [jnp.zeros((5, 128), F32)], axis=0)
    sel_mp[m] = sel_out[0]
    over_mp(lambda p: send(sel_out.at[0], sel_mp.at[m], 2, {"mp": p}))

    positions = lax.broadcasted_iota(jnp.int32, (1, BLOCK), 1) + c * BLOCK
    lanes = lax.broadcasted_iota(jnp.int32, (24, 128), 1)
    for s in range(SLOTS):
        usable = positions < lengths[s]
        for h in range(2):
            unit = s * 2 + h
            asks = jnp.concatenate(
                [rows_old[s * 24 + h * 8 : s * 24 + h * 8 + 8, :]]
                + [moved[s * MSG + ROW_Q + t * 16 + h * 8 : s * MSG + ROW_Q + t * 16 + h * 8 + 8, :] for t in range(2)],
                axis=0,
            )
            asked[unit] = asks
            fresh_rows[unit] = jnp.concatenate(
                [rows_old[s * 24 + 16 + h : s * 24 + 17 + h, :]]
                + [moved[s * MSG + ROW_F + t * 4 + h : s * MSG + ROW_F + t * 4 + h + 1, :] for t in range(2)]
                + [rows_old[s * 24 + 18 + h : s * 24 + 19 + h, :]]
                + [moved[s * MSG + ROW_F + t * 4 + 2 + h : s * MSG + ROW_F + t * 4 + 3 + h, :] for t in range(2)]
                + [jnp.zeros((2, 128), F32)],
                axis=0,
            )
            keys = key_ref[s, :, h * 128 : (h + 1) * 128]
            values = value_ref[s, :, h * 128 : (h + 1) * 128]
            scores = (
                lax.dot_general(asks.astype(BF16), keys, (((1,), (1,)), ((), ())), preferred_element_type=F32) * SCALE
            )
            scores = jnp.where(usable, scores, NEGATIVE)
            top = jnp.max(scores, axis=1, keepdims=True).astype(BF16).astype(F32)
            weights = jnp.where(usable, jnp.exp(scores - top), 0.0)
            total = jnp.sum(weights, axis=1, keepdims=True)
            mixed = jnp.dot(weights.astype(BF16), values, preferred_element_type=F32)
            high = total.astype(BF16).astype(F32)
            stats = jnp.where(lanes == 0, top, jnp.where(lanes == 1, high, total - high))
            part_out[unit] = jnp.concatenate([mixed, stats], axis=0).astype(BF16)
    part_in[c] = part_out[c]
    over_ctx(lambda p: send(part_out.at[p], part_in.at[c], 3, {"ctx": p}))

    arrived(sel_mp, 2, N_MP - 1)
    total = sel_mp[0]
    for k in range(1, N_MP):
        total += sel_mp[k]
    sel_sum[0] = total
    sel_ctx[c] = total
    over_ctx(lambda p: send(sel_sum.at[0], sel_ctx.at[c], 4, {"ctx": p}))

    arrived(part_in, 3, N_CTX - 1)
    asks = asked[c]
    fresh = fresh_rows[c]
    step_of = lax.broadcasted_iota(jnp.int32, (24, 1), 0) // 8
    parts = [part_in[k].astype(F32) for k in range(N_CTX)]
    tops = [part[24:48, 0:1] for part in parts]
    overall = tops[0]
    for k in range(1, N_CTX):
        overall = jnp.maximum(overall, tops[k])
    recents = []
    for u in range(3):
        score = jnp.sum(asks * fresh[u : u + 1, :], axis=1, keepdims=True) * SCALE
        score = jnp.where(step_of >= u, score, NEGATIVE)
        recents.append(score)
        overall = jnp.maximum(overall, score)
    numerator = jnp.zeros((24, 128), F32)
    denominator = jnp.zeros((24, 1), F32)
    for k in range(N_CTX):
        keep = jnp.exp(tops[k] - overall)
        numerator += parts[k][0:24, :] * keep
        denominator += (parts[k][24:48, 1:2] + parts[k][24:48, 2:3]) * keep
    for u in range(3):
        keep = jnp.where(step_of >= u, jnp.exp(recents[u] - overall), 0.0)
        numerator += fresh[3 + u : 4 + u, :] * keep
        denominator += keep
    done = jnp.concatenate([numerator / denominator, jnp.zeros((8, 128), F32)], axis=0).astype(BF16)
    fin_out[0] = done
    fin_in[c] = done
    over_ctx(lambda p: send(fin_out.at[0], fin_in.at[c], 5, {"ctx": p}))

    arrived(sel_ctx, 4, N_CTX - 1)
    total = sel_ctx[0]
    for k in range(1, N_CTX):
        total += sel_ctx[k]
    columns = jnp.transpose(total)
    sizes = [steps_ref[0]] + [moved_rows(ROW_S + (t - 1) * 4) for t in (1, 2)]
    gates = [inputs_ref[0, 1].astype(F32)] + [moved_rows(ROW_M + (t - 1) * 8 + 4) for t in (1, 2)]
    inputs = [filt[t, 0:SLOTS, :] for t in range(3)]
    for s in range(SLOTS):
        hidden = state_ref[s]
        for t in range(3):
            size = sizes[t][s : s + 1, :]
            into = columns[s * 32 : s * 32 + 16, t : t + 1]
            out = columns[s * 32 + 16 : s * 32 + 32, t : t + 1]
            hidden = jnp.exp(-size * rates) * hidden + into * (size * inputs[t][s : s + 1, :])
            scan_rows[t, s : s + 1, :] = jnp.sum(out * hidden, axis=0, keepdims=True)
    for t in range(3):
        result = (scan_rows[t, 0:SLOTS, :] + skip_ref[...] * inputs[t]) * (gates[t] * jax.nn.sigmoid(gates[t]))
        if t == 0:
            mam_ref[0] = result.astype(BF16)
        else:
            for ch in range(CHUNKS):
                mam_rows[pl.ds((t - 1) * 4 + ch, SLOTS, stride=8), :] = result[:, ch * 128 : (ch + 1) * 128]

    def leaves(s, p):
        return jnp.where(target_group[s] == p, 1.0, 0.0).astype(F32)

    def mam_message(p):
        total = mam_rows[0:8, :] * leaves(0, p)
        for s in range(1, SLOTS):
            total += mam_rows[s * 8 : (s + 1) * 8, :] * leaves(s, p)
        return total

    def mam_one(p):
        mam_out[p] = mam_message(p)
        send(mam_out.at[p], mam_in.at[d], 6, {"dp": p})

    over_dp(mam_one)
    mam_in[d] = mam_message(d)

    arrived(fin_in, 5, N_CTX - 1)
    finished = [fin_in[k].astype(F32) for k in range(N_CTX)]
    for s in range(SLOTS):
        for h in range(2):
            back_rows[s * 32 + h * 16 : s * 32 + h * 16 + 16, :] = finished[s * 2 + h][8:24, :]

    def ans_message(p):
        total = back_rows[0:32, :] * leaves(0, p)
        for s in range(1, SLOTS):
            total += back_rows[s * 32 : (s + 1) * 32, :] * leaves(s, p)
        return total.astype(BF16)

    def ans_one(p):
        ans_out[p] = ans_message(p)
        send(ans_out.at[p], ans_in.at[d], 7, {"dp": p})

    over_dp(ans_one)
    ans_in[d] = ans_message(d)
    for s in range(SLOTS):
        for h in range(2):
            rows_old[s * 24 + h * 8 : s * 24 + h * 8 + 8, :] = finished[s * 2 + h][0:8, :]
    for j in range(16):
        att_ref[0, :, j * 128 : (j + 1) * 128] = rows_old[pl.ds(j, SLOTS, stride=24), :].astype(BF16)

    arrived(mam_in, 6, N_DP - 1)
    for i in range(SLOTS):
        total = mam_in[0] * member[i, 0:1, :]
        for g in range(1, N_DP):
            total += mam_in[g] * member[i, g : g + 1, :]
        mam_rows[i * 8 : (i + 1) * 8, :] = total
    for t in (1, 2):
        for ch in range(CHUNKS):
            mam_ref[t, :, ch * 128 : (ch + 1) * 128] = mam_rows[
                pl.ds((t - 1) * 4 + ch, SLOTS, stride=8), :
            ].astype(BF16)
    arrived(ans_in, 7, N_DP - 1)
    for i in range(SLOTS):
        total = ans_in[0].astype(F32) * member[i, 0:1, :]
        for g in range(1, N_DP):
            total += ans_in[g].astype(F32) * member[i, g : g + 1, :]
        back_rows[i * 32 : (i + 1) * 32, :] = total
    for t in (1, 2):
        for h in range(2):
            for j in range(8):
                att_ref[t, :, (h * 8 + j) * 128 : (h * 8 + j + 1) * 128] = back_rows[
                    pl.ds(h * 16 + (t - 1) * 8 + j, SLOTS, stride=32), :
                ].astype(BF16)

    sent(table_in, 0, N_DP - 1)
    sent(ask_out, 1, N_DP - 1)
    sent(sel_mp, 2, N_MP - 1)
    sent(part_out, 3, N_CTX - 1)
    sent(sel_ctx, 4, N_CTX - 1)
    sent(fin_in, 5, N_CTX - 1)
    sent(mam_out, 6, N_DP - 1)
    sent(ans_out, 7, N_DP - 1)


def on_device(
    key_cache,
    value_cache,
    lengths,
    queries,
    fresh_pairs,
    recent_inputs,
    scan_state,
    mamba_inputs,
    step_sizes,
    filter_taps,
    filter_bias,
    decay_logs,
    skip_gain,
    select_weight,
    target_group,
    target_slot,
):
    smem = pl.BlockSpec(memory_space=pltpu.SMEM)
    vmem = pl.BlockSpec(memory_space=pltpu.VMEM)
    return pl.pallas_call(
        kernel,
        out_shape=(
            jax.ShapeDtypeStruct((3, SLOTS, 2048), BF16),
            jax.ShapeDtypeStruct((3, SLOTS, CHAN), BF16),
        ),
        in_specs=[smem] * 3 + [vmem] * 13,
        out_specs=(vmem, vmem),
        scratch_shapes=[
            pltpu.VMEM((1, 1, 128), jnp.int32),
            pltpu.VMEM((N_DP, 1, 128), jnp.int32),
            pltpu.VMEM((SLOTS, N_DP, 128), F32),
            pltpu.VMEM((SLOTS * MSG, 128), F32),
            pltpu.VMEM((SLOTS * 24, 128), F32),
            pltpu.VMEM((N_DP, MSG, 128), BF16),
            pltpu.VMEM((N_DP, MSG, 128), BF16),
            pltpu.VMEM((SLOTS * MSG, 128), F32),
            pltpu.VMEM((8, 24, 128), F32),
            pltpu.VMEM((8, 8, 128), F32),
            pltpu.VMEM((3, 8, CHAN), F32),
            pltpu.VMEM((1, 8, 128), F32),
            pltpu.VMEM((N_MP, 8, 128), F32),
            pltpu.VMEM((1, 8, 128), F32),
            pltpu.VMEM((N_CTX, 8, 128), F32),
            pltpu.VMEM((N_CTX, 48, 128), BF16),
            pltpu.VMEM((N_CTX, 48, 128), BF16),
            pltpu.VMEM((1, 32, 128), BF16),
            pltpu.VMEM((N_CTX, 32, 128), BF16),
            pltpu.VMEM((3, 8, CHAN), F32),
            pltpu.VMEM((SLOTS * 8, 128), F32),
            pltpu.VMEM((N_DP, 8, 128), F32),
            pltpu.VMEM((N_DP, 8, 128), F32),
            pltpu.VMEM((N_DP, 32, 128), BF16),
            pltpu.VMEM((N_DP, 32, 128), BF16),
            pltpu.VMEM((SLOTS * 32, 128), F32),
            pltpu.SemaphoreType.DMA((8,)),
            pltpu.SemaphoreType.DMA((8,)),
        ],
        compiler_params=pltpu.CompilerParams(
            collective_id=0, has_side_effects=True, vmem_limit_bytes=32 * 2**20
        ),
    )(
        lengths,
        target_group,
        target_slot,
        key_cache,
        value_cache,
        queries,
        fresh_pairs,
        recent_inputs,
        scan_state,
        mamba_inputs,
        step_sizes,
        filter_taps,
        filter_bias.reshape(1, CHAN),
        decay_logs,
        skip_gain.reshape(1, CHAN),
        select_weight,
    )


def solution(mesh):
    placed = (
        P("dp", "ctx", "mp"),
        P("dp", "ctx", "mp"),
        P("dp"),
        P(None, "dp", "mp"),
        P(None, None, "dp", "mp"),
        P("dp", None, ("ctx", "mp")),
        P("dp", None, ("ctx", "mp")),
        P(None, None, "dp", ("ctx", "mp")),
        P(None, "dp", ("ctx", "mp")),
        P(None, ("ctx", "mp")),
        P(("ctx", "mp")),
        P(None, ("ctx", "mp")),
        P(("ctx", "mp")),
        P(None, ("ctx", "mp")),
        P("dp"),
        P("dp"),
    )
    return jax.shard_map(
        on_device,
        mesh=mesh,
        in_specs=placed,
        out_specs=(P(None, "dp", "mp"), P(None, "dp", ("ctx", "mp"))),
        check_vma=False,
    )
```

time: 446 us -> 58.4 us (0.13)
  the two profiles are of different devices: /device:TPU:16 before, /device:TPU:1 now
where the time goes in v1:
time: 58.4 us; the launch traced here: 57.7 us
  Pallas kernels  47.6 us (82%)
  local copies, waits for them, and re-layouts  9.41 us (16%)
  between operations  0.75 us (1%)
    pallas_call x1, Pallas kernels, on_device(): pl.pallas_call(kernel, out_shape=(jax.ShapeDtypeStruct((3, SLOTS, 2048),...  47.6 us
    unnamed x33, local copies, waits for them, and re-layouts  9.41 us

profile of v1, /device:TPU:1, one launch (start us, length us, event | category | flops | bytes accessed | tf_op | source)
XLA Modules:
  0.0 57.7 jit_solution(6150865731441824627)
XLA Ops:
  0.6 0.0 copy-start.6
  0.6 0.0 copy-start.9
  0.7 0.0 copy-start.10
  0.7 0.0 copy-start.12
  0.7 0.0 copy-start.13
  0.7 0.0 copy-start.14
  0.7 0.7 %copy.18.recent_ref = bf16[4,3,512]{2,1,0:T(4,128)(2,1)S(1)} copy(bf16[4,3,512]{2,0,1:T(4,128)(2,1)} %param.21) | data formatting | bytes 24576 | tf_op args[5]
  1.4 0.0 copy-done.9
  1.5 0.0 copy-done.10
  1.5 0.0 copy-done.12
  1.5 0.0 copy-done.13
  1.5 0.0 copy-start
  1.5 1.0 %copy-done = bf16[4,256,256]{2,1,0:T(8,128)(2,1)S(1)} copy-done((bf16[4,256,256]{2,1,0:T(8,128)(2,1)S(1)}, bf16[4,256,256]{2,1,0:T(8,128)(2,1)}, u32[]{:S(2)}) %copy-start) | copy-done | bytes 524312
  2.5 1.0 %copy-done.1 = bf16[4,256,256]{2,1,0:T(8,128)(2,1)S(1)} copy-done((bf16[4,256,256]{2,1,0:T(8,128)(2,1)S(1)}, bf16[4,256,256]{2,1,0:T(8,128)(2,1)}, u32[]{:S(2)}) %copy-start.1) | copy-done | bytes 524312
  3.6 0.9 %copy-done.2 = f32[4,16,512]{2,1,0:T(8,128)S(1)} copy-done((f32[4,16,512]{2,1,0:T(8,128)S(1)}, f32[4,16,512]{2,1,0:T(8,128)}, u32[]{:S(2)}) %copy-start.2) | copy-done | bytes 131096
  4.5 0.8 %copy-done.3 = bf16[3,4,2048]{2,1,0:T(4,128)(2,1)S(1)} copy-done((bf16[3,4,2048]{2,1,0:T(4,128)(2,1)S(1)}, bf16[3,4,2048]{2,1,0:T(4,128)(2,1)}, u32[]{:S(2)}) %copy-start.3) | copy-done | bytes 49176
  5.3 0.8 %copy-done.4 = f32[16,512]{1,0:T(8,128)S(1)} copy-done((f32[16,512]{1,0:T(8,128)S(1)}, f32[16,512]{1,0:T(8,128)}, u32[]{:S(2)}) %copy-start.4) | copy-done | bytes 32792
  6.0 0.8 %copy-done.5 = bf16[32,512]{1,0:T(8,128)(2,1)S(1)} copy-done((bf16[32,512]{1,0:T(8,128)(2,1)S(1)}, bf16[32,512]{1,0:T(8,128)(2,1)}, u32[]{:S(2)}) %copy-start.5) | copy-done | bytes 32792
  6.8 0.7 %copy-done.7 = f32[3,4,512]{2,1,0:T(4,128)S(1)} copy-done((f32[3,4,512]{2,1,0:T(4,128)S(1)}, f32[3,4,512]{2,1,0:T(4,128)}, u32[]{:S(2)}) %copy-start.7) | copy-done | bytes 24600
  7.5 0.7 %copy-done.8 = bf16[3,2,4,256]{3,2,1,0:T(4,128)(2,1)S(1)} copy-done((bf16[3,2,4,256]{3,2,1,0:T(4,128)(2,1)S(1)}, bf16[3,2,4,256]{3,2,1,0:T(4,128)(2,1)}, u32[]{:S(2)}) %copy-start.8) | copy-done | bytes 12312
  8.3 0.7 %copy-done.11 = f32[512]{0:T(512)S(1)} copy-done((f32[512]{0:T(512)S(1)}, f32[512]{0:T(512)}, u32[]{:S(2)}) %copy-start.11) | copy-done | bytes 2072
  8.9 47.6 %shard_map.167 = (bf16[3,4,2048]{2,1,0:T(4,128)(2,1)S(1)}, bf16[3,4,512]{2,1,0:T(4,128)(2,1)S(1)}) custom-call(s32[4]{0:T(128)S(1)} %copy-done.12, s32[4]{0:T(128)S(1)} %copy-done.13, s32[4]{0:T(128)S(1)} %copy-done.14, bf16[4,256,256]{2,1,0:T(8,128)(2,1)S(1)} %copy-done, bf16[4,256,256]{2,1,0:T(8,128)(2,1)S(1)} %copy-done.1, ...), custom_call_target="tpu_custom_call" | custom-call | tf_op jit(solution)/shard_map/pallas_call | solution.py:411
  56.5 0.6 %copy.21 = bf16[3,4,2048]{2,1,0:T(4,128)(2,1)} copy(bf16[3,4,2048]{2,1,0:T(4,128)(2,1)S(1)} %get-tuple-element.4) | data formatting | bytes 98304
  57.1 0.6 %copy.22 = bf16[3,4,512]{2,1,0:T(4,128)(2,1)} copy(bf16[3,4,512]{2,1,0:T(4,128)(2,1)S(1)} %get-tuple-element.5) | data formatting | bytes 24576
  (10 shorter events, 0.0 us)
Async XLA Ops:
  0.6 0.8 %copy-start.6 = (bf16[3,2,4,512]{3,2,1,0:T(4,128)(2,1)S(1)}, bf16[3,2,4,512]{3,2,1,0:T(4,128)(2,1)}, u32[]{:S(2)}) copy-start(bf16[3,2,4,512]{3,2,1,0:T(4,128)(2,1)} %inputs_ref.1) | copy-start | bytes 73732
  0.6 0.8 %copy-start.9 = (bf16[4,512]{1,0:T(4,128)(2,1)S(1)}, bf16[4,512]{1,0:T(4,128)(2,1)}, u32[]{:S(2)}) copy-start(bf16[4,512]{1,0:T(4,128)(2,1)} %taps_ref.1) | copy-start | bytes 12292
  0.7 0.8 %copy-start.10 = (f32[512]{0:T(512)S(1)}, f32[512]{0:T(512)}, u32[]{:S(2)}) copy-start(f32[512]{0:T(512)} %param.26) | copy-start | bytes 6148
  0.7 0.8 %copy-start.12 = (s32[4]{0:T(128)S(1)}, s32[4]{0:T(128)}, u32[]{:S(2)}) copy-start(s32[4]{0:T(128)} %lengths.1) | copy-start | bytes 52
  0.7 0.8 %copy-start.13 = (s32[4]{0:T(128)S(1)}, s32[4]{0:T(128)}, u32[]{:S(2)}) copy-start(s32[4]{0:T(128)} %target_group.1) | copy-start | bytes 52
  0.7 0.8 %copy-start.14 = (s32[4]{0:T(128)S(1)}, s32[4]{0:T(128)}, u32[]{:S(2)}) copy-start(s32[4]{0:T(128)} %target_slot.1) | copy-start | bytes 52
  1.5 1.0 %copy-start = (bf16[4,256,256]{2,1,0:T(8,128)(2,1)S(1)}, bf16[4,256,256]{2,1,0:T(8,128)(2,1)}, u32[]{:S(2)}) copy-start(bf16[4,256,256]{2,1,0:T(8,128)(2,1)} %key_ref.1) | copy-start | bytes 1572868
  2.5 1.0 %copy-start.1 = (bf16[4,256,256]{2,1,0:T(8,128)(2,1)S(1)}, bf16[4,256,256]{2,1,0:T(8,128)(2,1)}, u32[]{:S(2)}) copy-start(bf16[4,256,256]{2,1,0:T(8,128)(2,1)} %value_ref.1) | copy-start | bytes 1572868
  3.6 0.9 %copy-start.2 = (f32[4,16,512]{2,1,0:T(8,128)S(1)}, f32[4,16,512]{2,1,0:T(8,128)}, u32[]{:S(2)}) copy-start(f32[4,16,512]{2,1,0:T(8,128)} %state_ref.1) | copy-start | bytes 393220
  4.5 0.8 %copy-start.3 = (bf16[3,4,2048]{2,1,0:T(4,128)(2,1)S(1)}, bf16[3,4,2048]{2,1,0:T(4,128)(2,1)}, u32[]{:S(2)}) copy-start(bf16[3,4,2048]{2,1,0:T(4,128)(2,1)} %query_ref.1) | copy-start | bytes 147460
  5.3 0.8 %copy-start.4 = (f32[16,512]{1,0:T(8,128)S(1)}, f32[16,512]{1,0:T(8,128)}, u32[]{:S(2)}) copy-start(f32[16,512]{1,0:T(8,128)} %decay_ref.1) | copy-start | bytes 98308
  6.0 0.8 %copy-start.5 = (bf16[32,512]{1,0:T(8,128)(2,1)S(1)}, bf16[32,512]{1,0:T(8,128)(2,1)}, u32[]{:S(2)}) copy-start(bf16[32,512]{1,0:T(8,128)(2,1)} %select_ref.1) | copy-start | bytes 98308
  6.8 0.7 %copy-start.7 = (f32[3,4,512]{2,1,0:T(4,128)S(1)}, f32[3,4,512]{2,1,0:T(4,128)}, u32[]{:S(2)}) copy-start(f32[3,4,512]{2,1,0:T(4,128)} %steps_ref.1) | copy-start | bytes 73732
  7.5 0.7 %copy-start.8 = (bf16[3,2,4,256]{3,2,1,0:T(4,128)(2,1)S(1)}, bf16[3,2,4,256]{3,2,1,0:T(4,128)(2,1)}, u32[]{:S(2)}) copy-start(bf16[3,2,4,256]{3,2,1,0:T(4,128)(2,1)} %fresh_ref.1) | copy-start | bytes 36868
  8.2 0.7 %copy-start.11 = (f32[512]{0:T(512)S(1)}, f32[512]{0:T(512)}, u32[]{:S(2)}) copy-start(f32[512]{0:T(512)} %param.28) | copy-start | bytes 6148

commit v2 on v1

--- a/solution.py
+++ b/solution.py
@@ -26,27 +26,23 @@
 ROW_Q = 0
 ROW_F = 32
 ROW_M = 40
-ROW_S = 56
-MSG = 64
-
-
-def kernel(
-    lengths,
-    target_group,
-    target_slot,
-    key_ref,
-    value_ref,
-    query_ref,
-    fresh_ref,
-    recent_ref,
-    state_ref,
-    inputs_ref,
-    steps_ref,
-    taps_ref,
-    bias_ref,
-    decay_ref,
-    skip_ref,
-    select_ref,
+MSG = 48
+ROW_S = 48
+ROWS = 56
+
+LOAD_ORDER = (1, 2, 5, 6, 9, 10, 7, 11, 12, 0, 15, 3, 4, 8, 13, 14)
+
+
+def kernel(*refs):
+    operands, (att_ref, mam_ref), rest = refs[:16], refs[16:18], refs[18:]
+    local, in_sem, rest = rest[:16], rest[16], rest[17:]
+    run(operands, local, in_sem, att_ref, mam_ref, *rest)
+
+
+def run(
+    operands,
+    local,
+    in_sem,
     att_ref,
     mam_ref,
     table_out,
@@ -56,7 +52,10 @@
     rows_old,
     ask_out,
     ask_in,
+    size_out,
+    size_in,
     moved,
+    moved_sizes,
     asked,
     fresh_rows,
     filt,
@@ -78,6 +77,12 @@
     send_sem,
     recv_sem,
 ):
+    (lengths, target_group, target_slot, key_ref, value_ref, query_ref, fresh_ref, recent_ref) = local[:8]
+    (state_ref, inputs_ref, steps_ref, taps_ref, bias_ref, decay_ref, skip_ref, select_ref) = local[8:]
+    loads = [pltpu.make_async_copy(operands[k], local[k], in_sem.at[k]) for k in range(16)]
+    for k in LOAD_ORDER:
+        loads[k].start()
+
     d = lax.axis_index("dp")
     c = lax.axis_index("ctx")
     m = lax.axis_index("mp")
@@ -126,6 +131,8 @@
     over_ctx(lambda p: pl.semaphore_signal(barrier, inc=1, device_id={"ctx": p}, device_id_type=MESH))
     over_mp(lambda p: pl.semaphore_signal(barrier, inc=1, device_id={"mp": p}, device_id_type=MESH))
 
+    loads[1].wait()
+    loads[2].wait()
     lane = lax.broadcasted_iota(jnp.int32, (1, 128), 1)
     landing = jnp.full((1, 128), -1, jnp.int32)
     for s in range(SLOTS):
@@ -136,21 +143,22 @@
 
     over_dp(lambda p: send(table_out.at[0], table_in.at[d], 0, {"dp": p}))
 
+    for k in (5, 6, 9, 10):
+        loads[k].wait()
     for t in (1, 2):
         q = query_ref[t].astype(F32)
         for j in range(16):
-            rows_new[pl.ds(ROW_Q + (t - 1) * 16 + j, SLOTS, stride=MSG), :] = q[:, j * 128 : (j + 1) * 128]
+            rows_new[pl.ds(ROW_Q + (t - 1) * 16 + j, SLOTS, stride=ROWS), :] = q[:, j * 128 : (j + 1) * 128]
         for kv in range(2):
             f = fresh_ref[t, kv].astype(F32)
             for h in range(2):
-                rows_new[pl.ds(ROW_F + (t - 1) * 4 + kv * 2 + h, SLOTS, stride=MSG), :] = f[:, h * 128 : (h + 1) * 128]
-        for w in range(2):
-            x = inputs_ref[t, w].astype(F32)
-            for ch in range(CHUNKS):
-                rows_new[pl.ds(ROW_M + (t - 1) * 8 + w * 4 + ch, SLOTS, stride=MSG), :] = x[:, ch * 128 : (ch + 1) * 128]
+                rows_new[pl.ds(ROW_F + (t - 1) * 4 + kv * 2 + h, SLOTS, stride=ROWS), :] = f[:, h * 128 : (h + 1) * 128]
+        x = inputs_ref[t, 0].astype(F32)
+        for ch in range(CHUNKS):
+            rows_new[pl.ds(ROW_M + (t - 1) * 4 + ch, SLOTS, stride=ROWS), :] = x[:, ch * 128 : (ch + 1) * 128]
         x = steps_ref[t]
         for ch in range(CHUNKS):
-            rows_new[pl.ds(ROW_S + (t - 1) * 4 + ch, SLOTS, stride=MSG), :] = x[:, ch * 128 : (ch + 1) * 128]
+            rows_new[pl.ds(ROW_S + (t - 1) * 4 + ch, SLOTS, stride=ROWS), :] = x[:, ch * 128 : (ch + 1) * 128]
     q = query_ref[0].astype(F32)
     for j in range(16):
         rows_old[pl.ds(j, SLOTS, stride=24), :] = q[:, j * 128 : (j + 1) * 128]
@@ -165,23 +173,31 @@
         hit = jnp.where(table == d * SLOTS + i, 1.0, 0.0).astype(F32)
         member[i] = jnp.broadcast_to(jnp.max(hit, axis=1, keepdims=True), (N_DP, 128))
 
-    def ask(p):
-        total = rows_new[0:MSG, :] * member[0, pl.ds(p, 1), :]
+    def chosen(p, first, last):
+        total = rows_new[first:last, :] * member[0, pl.ds(p, 1), :]
         for i in range(1, SLOTS):
-            total += rows_new[i * MSG : (i + 1) * MSG, :] * member[i, pl.ds(p, 1), :]
-        return total.astype(BF16)
+            total += rows_new[i * ROWS + first : i * ROWS + last, :] * member[i, pl.ds(p, 1), :]
+        return total
 
     def ask_one(p):
-        ask_out[p] = ask(p)
+        ask_out[p] = chosen(p, 0, MSG).astype(BF16)
         send(ask_out.at[p], ask_in.at[d], 1, {"dp": p})
 
     over_dp(ask_one)
-    ask_in[d] = ask(d)
-
+    ask_in[d] = chosen(d, 0, MSG).astype(BF16)
+
+    def size_one(p):
+        size_out[p] = chosen(p, ROW_S, ROWS)
+        send(size_out.at[p], size_in.at[d], 8, {"dp": p})
+
+    over_dp(size_one)
+    size_in[d] = chosen(d, ROW_S, ROWS)
+
+    for k in (7, 11, 12):
+        loads[k].wait()
     taps = taps_ref[...].astype(F32)
     bias = bias_ref[...]
-    recent = recent_ref[...].astype(F32)
-    window = [recent[:, k, :] for k in range(3)] + [inputs_ref[0, 0].astype(F32)]
+    window = [recent_ref[k].astype(F32) for k in range(3)] + [inputs_ref[0, 0].astype(F32)]
 
     def filtered(parts):
         total = parts[0] * taps[0:1, :]
@@ -191,18 +207,18 @@
         return (total * jax.nn.sigmoid(total)).astype(BF16).astype(F32)
 
     filt[0, 0:SLOTS, :] = filtered(window)
-    rates = jnp.exp(decay_ref[...])
 
     arrived(ask_in, 1, N_DP - 1)
     for s in range(SLOTS):
         moved[s * MSG : (s + 1) * MSG, :] = ask_in[target_group[s]].astype(F32)
 
-    def moved_rows(row):
-        return jnp.concatenate([moved[pl.ds(row + ch, SLOTS, stride=MSG), :] for ch in range(CHUNKS)], axis=1)
+    def lined_up(ref, row, stride):
+        return jnp.concatenate([ref[pl.ds(row + ch, SLOTS, stride=stride), :] for ch in range(CHUNKS)], axis=1)
 
     for t in (1, 2):
-        window = window[1:] + [moved_rows(ROW_M + (t - 1) * 8)]
+        window = window[1:] + [lined_up(moved, ROW_M + (t - 1) * 4, MSG)]
         filt[t, 0:SLOTS, :] = filtered(window)
+    loads[15].wait()
     weight = select_ref[...]
     weight = jnp.concatenate([weight] * SLOTS, axis=0)
     own = lax.broadcasted_iota(jnp.int32, (8, 128), 1) // 32 == lax.broadcasted_iota(jnp.int32, (8, 128), 0)
@@ -216,6 +232,8 @@
     sel_mp[m] = sel_out[0]
     over_mp(lambda p: send(sel_out.at[0], sel_mp.at[m], 2, {"mp": p}))
 
+    for k in (0, 3, 4):
+        loads[k].wait()
     positions = lax.broadcasted_iota(jnp.int32, (1, BLOCK), 1) + c * BLOCK
     lanes = lax.broadcasted_iota(jnp.int32, (24, 128), 1)
     for s in range(SLOTS):
@@ -295,9 +313,19 @@
     for k in range(1, N_CTX):
         total += sel_ctx[k]
     columns = jnp.transpose(total)
-    sizes = [steps_ref[0]] + [moved_rows(ROW_S + (t - 1) * 4) for t in (1, 2)]
-    gates = [inputs_ref[0, 1].astype(F32)] + [moved_rows(ROW_M + (t - 1) * 8 + 4) for t in (1, 2)]
+    arrived(size_in, 8, N_DP - 1)
+    for s in range(SLOTS):
+        moved_sizes[s * 8 : (s + 1) * 8, :] = size_in[target_group[s]]
+    for k in (8, 13, 14):
+        loads[k].wait()
+    rates = jnp.exp(decay_ref[...])
+    sizes = [steps_ref[0]] + [lined_up(moved_sizes, (t - 1) * 4, 8) for t in (1, 2)]
     inputs = [filt[t, 0:SLOTS, :] for t in range(3)]
+
+    def gated(result, t):
+        gate = inputs_ref[t, 1].astype(F32)
+        return (result * (gate * jax.nn.sigmoid(gate))).astype(BF16)
+
     for s in range(SLOTS):
         hidden = state_ref[s]
         for t in range(3):
@@ -307,9 +335,9 @@
             hidden = jnp.exp(-size * rates) * hidden + into * (size * inputs[t][s : s + 1, :])
             scan_rows[t, s : s + 1, :] = jnp.sum(out * hidden, axis=0, keepdims=True)
     for t in range(3):
-        result = (scan_rows[t, 0:SLOTS, :] + skip_ref[...] * inputs[t]) * (gates[t] * jax.nn.sigmoid(gates[t]))
+        result = scan_rows[t, 0:SLOTS, :] + skip_ref[...] * inputs[t]
         if t == 0:
-            mam_ref[0] = result.astype(BF16)
+            mam_ref[0] = gated(result, 0)
         else:
             for ch in range(CHUNKS):
                 mam_rows[pl.ds((t - 1) * 4 + ch, SLOTS, stride=8), :] = result[:, ch * 128 : (ch + 1) * 128]
@@ -361,10 +389,7 @@
             total += mam_in[g] * member[i, g : g + 1, :]
         mam_rows[i * 8 : (i + 1) * 8, :] = total
     for t in (1, 2):
-        for ch in range(CHUNKS):
-            mam_ref[t, :, ch * 128 : (ch + 1) * 128] = mam_rows[
-                pl.ds((t - 1) * 4 + ch, SLOTS, stride=8), :
-            ].astype(BF16)
+        mam_ref[t] = gated(lined_up(mam_rows, (t - 1) * 4, 8), t)
     arrived(ans_in, 7, N_DP - 1)
     for i in range(SLOTS):
         total = ans_in[0].astype(F32) * member[i, 0:1, :]
@@ -380,6 +405,7 @@
 
     sent(table_in, 0, N_DP - 1)
     sent(ask_out, 1, N_DP - 1)
+    sent(size_out, 8, N_DP - 1)
     sent(sel_mp, 2, N_MP - 1)
     sent(part_out, 3, N_CTX - 1)
     sent(sel_ctx, 4, N_CTX - 1)
@@ -406,25 +432,48 @@
     target_group,
     target_slot,
 ):
-    smem = pl.BlockSpec(memory_space=pltpu.SMEM)
     vmem = pl.BlockSpec(memory_space=pltpu.VMEM)
+    operands = (
+        lengths,
+        target_group,
+        target_slot,
+        key_cache,
+        value_cache,
+        queries,
+        fresh_pairs,
+        jnp.swapaxes(recent_inputs, 0, 1),
+        scan_state,
+        mamba_inputs,
+        step_sizes,
+        filter_taps,
+        filter_bias.reshape(1, CHAN),
+        decay_logs,
+        skip_gain.reshape(1, CHAN),
+        select_weight,
+    )
     return pl.pallas_call(
         kernel,
         out_shape=(
             jax.ShapeDtypeStruct((3, SLOTS, 2048), BF16),
             jax.ShapeDtypeStruct((3, SLOTS, CHAN), BF16),
         ),
-        in_specs=[smem] * 3 + [vmem] * 13,
+        in_specs=[pl.BlockSpec(memory_space=pltpu.HBM)] * 16,
         out_specs=(vmem, vmem),
-        scratch_shapes=[
+        scratch_shapes=[pltpu.SMEM((SLOTS,), jnp.int32)] * 3
+        + [pltpu.VMEM(x.shape, x.dtype) for x in operands[3:]]
+        + [
+            pltpu.SemaphoreType.DMA((16,)),
             pltpu.VMEM((1, 1, 128), jnp.int32),
             pltpu.VMEM((N_DP, 1, 128), jnp.int32),
             pltpu.VMEM((SLOTS, N_DP, 128), F32),
-            pltpu.VMEM((SLOTS * MSG, 128), F32),
+            pltpu.VMEM((SLOTS * ROWS, 128), F32),
             pltpu.VMEM((SLOTS * 24, 128), F32),
             pltpu.VMEM((N_DP, MSG, 128), BF16),
             pltpu.VMEM((N_DP, MSG, 128), BF16),
+            pltpu.VMEM((N_DP, 8, 128), F32),
+            pltpu.VMEM((N_DP, 8, 128), F32),
             pltpu.VMEM((SLOTS * MSG, 128), F32),
+            pltpu.VMEM((SLOTS * 8, 128), F32),
             pltpu.VMEM((8, 24, 128), F32),
             pltpu.VMEM((8, 8, 128), F32),
             pltpu.VMEM((3, 8, CHAN), F32),
@@ -443,30 +492,13 @@
             pltpu.VMEM((N_DP, 32, 128), BF16),
             pltpu.VMEM((N_DP, 32, 128), BF16),
             pltpu.VMEM((SLOTS * 32, 128), F32),
-            pltpu.SemaphoreType.DMA((8,)),
-            pltpu.SemaphoreType.DMA((8,)),
+            pltpu.SemaphoreType.DMA((9,)),
+            pltpu.SemaphoreType.DMA((9,)),
         ],
         compiler_params=pltpu.CompilerParams(
-            collective_id=0, has_side_effects=True, vmem_limit_bytes=32 * 2**20
+            collective_id=0, has_side_effects=True, vmem_limit_bytes=60 * 2**20
         ),
-    )(
-        lengths,
-        target_group,
-        target_slot,
-        key_cache,
-        value_cache,
-        queries,
-        fresh_pairs,
-        recent_inputs,
-        scan_state,
-        mamba_inputs,
-        step_sizes,
-        filter_taps,
-        filter_bias.reshape(1, CHAN),
-        decay_logs,
-        skip_gain.reshape(1, CHAN),
-        select_weight,
-    )
+    )(*operands)
 
 
 def solution(mesh):

time: 58.4 us -> 51.1 us (0.88)
  local copies, waits for them, and re-layouts: 9.41 us -> 2.05 us
  Pallas kernels: 47.6 us -> 48.2 us
    unnamed x33 -> x4, local copies, waits for them, and re-layouts: 9.41 us -> 2.05 us
    pallas_call x1, Pallas kernels: 47.6 us -> 48.2 us  [on_device(): pl.pallas_call(kernel, out_shape=(jax.ShapeDtypeStruct((3, SLOTS, 2048),...]
where the time goes in v2:
time: 51.1 us; the launch traced here: 50.9 us
  Pallas kernels  48.2 us (94%)
  local copies, waits for them, and re-layouts  2.05 us (4%)
  between operations  0.65 us (1%)
    pallas_call x1, Pallas kernels, on_device(): pl.pallas_call(kernel, out_shape=(jax.ShapeDtypeStruct((3, SLOTS, 2048),...  48.2 us
    unnamed x4, local copies, waits for them, and re-layouts  2.05 us

profile of v2, /device:TPU:1, one launch (start us, length us, event | category | flops | bytes accessed | tf_op | source)
XLA Modules:
  0.0 50.9 jit_solution(8052464692145764200)
XLA Ops:
  0.6 48.2 %shard_map.167 = (bf16[3,4,2048]{2,1,0:T(4,128)(2,1)}, bf16[3,4,512]{2,1,0:T(4,128)(2,1)}) custom-call(s32[4]{0:T(128)} %refs_0_.1, s32[4]{0:T(128)} %refs_1_.1, s32[4]{0:T(128)} %refs_2_.1, bf16[4,256,256]{2,1,0:T(8,128)(2,1)} %refs_3_.1, bf16[4,256,256]{2,1,0:T(8,128)(2,1)} %refs_4_.1, bf16[3,4,2048]{2,1,0:T(4,128)(2,1)} %refs_5_.1, ...), custom_call_target="tpu_custom_call" | custom-call | tf_op jit(solution)/shard_map/pallas_call | solution.py:454
  48.9 0.0 copy-start
  48.9 1.4 %copy.20 = bf16[3,4,2048]{2,1,0:T(4,128)(2,1)} copy(bf16[3,4,2048]{2,1,0:T(4,128)(2,1)} %get-tuple-element.4) | data formatting | bytes 98304
  50.3 0.0 copy-done
  50.3 0.6 %copy.21 = bf16[3,4,512]{2,1,0:T(4,128)(2,1)} copy(bf16[3,4,512]{2,1,0:T(4,128)(2,1)S(1)} %copy-done) | data formatting | bytes 24576
Async XLA Ops:
  48.9 1.5 %copy-start = (bf16[3,4,512]{2,1,0:T(4,128)(2,1)S(1)}, bf16[3,4,512]{2,1,0:T(4,128)(2,1)}, u32[]{:S(2)}) copy-start(bf16[3,4,512]{2,1,0:T(4,128)(2,1)} %get-tuple-element.5) | copy-start | bytes 36868

commit v3 on v2

--- a/solution.py
+++ b/solution.py
@@ -26,7 +26,6 @@
 ROW_Q = 0
 ROW_F = 32
 ROW_M = 40
-MSG = 48
 ROW_S = 48
 ROWS = 56
 
@@ -52,6 +51,8 @@
     rows_old,
     ask_out,
     ask_in,
+    new_out,
+    new_in,
     size_out,
     size_in,
     moved,
@@ -67,6 +68,8 @@
     part_in,
     fin_out,
     fin_in,
+    one_out,
+    one_in,
     scan_rows,
     mam_rows,
     mam_out,
@@ -89,24 +92,27 @@
 
     def over_dp(fn):
         def body(k, carry):
-            fn(lax.rem(d + k, N_DP))
+            away = N_DP // 2 + jnp.where(k % 2 == 1, -((k + 1) // 2), k // 2)
+            fn(lax.rem(d + away, N_DP))
             return carry
 
-        lax.fori_loop(1, N_DP, body, 0)
+        lax.fori_loop(0, N_DP - 1, body, 0)
 
     def over_ctx(fn):
         def body(k, carry):
-            fn(lax.rem(c + k, N_CTX))
+            away = N_CTX // 2 + jnp.where(k % 2 == 1, -((k + 1) // 2), k // 2)
+            fn(lax.rem(c + away, N_CTX))
             return carry
 
-        lax.fori_loop(1, N_CTX, body, 0)
+        lax.fori_loop(0, N_CTX - 1, body, 0)
 
     def over_mp(fn):
         def body(k, carry):
-            fn(lax.rem(m + k, N_MP))
+            away = N_MP // 2 + jnp.where(k % 2 == 1, -((k + 1) // 2), k // 2)
+            fn(lax.rem(m + away, N_MP))
             return carry
 
-        lax.fori_loop(1, N_MP, body, 0)
+        lax.fori_loop(0, N_MP - 1, body, 0)
 
     def send(src, dst, phase, device):
         pltpu.make_async_remote_copy(
@@ -179,19 +185,17 @@
             total += rows_new[i * ROWS + first : i * ROWS + last, :] * member[i, pl.ds(p, 1), :]
         return total
 
-    def ask_one(p):
-        ask_out[p] = chosen(p, 0, MSG).astype(BF16)
-        send(ask_out.at[p], ask_in.at[d], 1, {"dp": p})
-
-    over_dp(ask_one)
-    ask_in[d] = chosen(d, 0, MSG).astype(BF16)
-
-    def size_one(p):
-        size_out[p] = chosen(p, ROW_S, ROWS)
-        send(size_out.at[p], size_in.at[d], 8, {"dp": p})
-
-    over_dp(size_one)
-    size_in[d] = chosen(d, ROW_S, ROWS)
+    def message(first, last, out, into, phase):
+        def one(p):
+            out[p] = chosen(p, first, last).astype(out.dtype)
+            send(out.at[p], into.at[d], phase, {"dp": p})
+
+        over_dp(one)
+        into[d] = chosen(d, first, last).astype(out.dtype)
+
+    message(ROW_Q, ROW_F, ask_out, ask_in, 1)
+    message(ROW_F, ROW_S, new_out, new_in, 8)
+    message(ROW_S, ROWS, size_out, size_in, 9)
 
     for k in (7, 11, 12):
         loads[k].wait()
@@ -208,19 +212,59 @@
 
     filt[0, 0:SLOTS, :] = filtered(window)
 
+    for k in (0, 3, 4, 15):
+        loads[k].wait()
+    positions = lax.broadcasted_iota(jnp.int32, (24, BLOCK), 1) + c * BLOCK
+    weight = select_ref[...]
+    weight = jnp.concatenate([weight] * SLOTS, axis=0)
+
     arrived(ask_in, 1, N_DP - 1)
     for s in range(SLOTS):
-        moved[s * MSG : (s + 1) * MSG, :] = ask_in[target_group[s]].astype(F32)
+        queries = ask_in[target_group[s]].astype(F32)
+        for h in range(2):
+            asked[s * 2 + h] = jnp.concatenate(
+                [rows_old[s * 24 + h * 8 : s * 24 + h * 8 + 8, :]]
+                + [queries[t * 16 + h * 8 : t * 16 + h * 8 + 8, :] for t in range(2)],
+                axis=0,
+            )
+    units = [(s, h) for s in range(SLOTS) for h in range(2)]
+    scores = [
+        lax.dot_general(
+            asked[s * 2 + h].astype(BF16),
+            key_ref[s, :, h * 128 : (h + 1) * 128],
+            (((1,), (1,)), ((), ())),
+            preferred_element_type=F32,
+        )
+        * SCALE
+        for s, h in units
+    ]
+    usable = [positions < lengths[s] for s, h in units]
+    scores = [jnp.where(usable[k], scores[k], NEGATIVE) for k in range(8)]
+    tops = [jnp.max(x, axis=1, keepdims=True).astype(BF16).astype(F32) for x in scores]
+    weights = [jnp.where(usable[k], jnp.exp(scores[k] - tops[k]), 0.0) for k in range(8)]
+    totals = [jnp.sum(x, axis=1, keepdims=True) for x in weights]
+    mixed = [
+        jnp.dot(weights[s * 2 + h].astype(BF16), value_ref[s, :, h * 128 : (h + 1) * 128], preferred_element_type=F32)
+        for s, h in units
+    ]
+    lanes = lax.broadcasted_iota(jnp.int32, (24, 128), 1)
+    for k in range(8):
+        high = totals[k].astype(BF16).astype(F32)
+        stats = jnp.where(lanes == 0, tops[k], jnp.where(lanes == 1, high, totals[k] - high))
+        part_out[k] = jnp.concatenate([mixed[k], stats], axis=0).astype(BF16)
+    part_in[c] = part_out[c]
+    over_ctx(lambda p: send(part_out.at[p], part_in.at[c], 3, {"ctx": p}))
+
+    arrived(new_in, 8, N_DP - 1)
+    for s in range(SLOTS):
+        moved[s * 16 : s * 16 + 16, :] = new_in[target_group[s]].astype(F32)
 
     def lined_up(ref, row, stride):
         return jnp.concatenate([ref[pl.ds(row + ch, SLOTS, stride=stride), :] for ch in range(CHUNKS)], axis=1)
 
     for t in (1, 2):
-        window = window[1:] + [lined_up(moved, ROW_M + (t - 1) * 4, MSG)]
+        window = window[1:] + [lined_up(moved, 8 + (t - 1) * 4, 16)]
         filt[t, 0:SLOTS, :] = filtered(window)
-    loads[15].wait()
-    weight = select_ref[...]
-    weight = jnp.concatenate([weight] * SLOTS, axis=0)
     own = lax.broadcasted_iota(jnp.int32, (8, 128), 1) // 32 == lax.broadcasted_iota(jnp.int32, (8, 128), 0)
     picks = []
     for t in range(3):
@@ -232,43 +276,16 @@
     sel_mp[m] = sel_out[0]
     over_mp(lambda p: send(sel_out.at[0], sel_mp.at[m], 2, {"mp": p}))
 
-    for k in (0, 3, 4):
-        loads[k].wait()
-    positions = lax.broadcasted_iota(jnp.int32, (1, BLOCK), 1) + c * BLOCK
-    lanes = lax.broadcasted_iota(jnp.int32, (24, 128), 1)
-    for s in range(SLOTS):
-        usable = positions < lengths[s]
+    for s in range(SLOTS):
         for h in range(2):
-            unit = s * 2 + h
-            asks = jnp.concatenate(
-                [rows_old[s * 24 + h * 8 : s * 24 + h * 8 + 8, :]]
-                + [moved[s * MSG + ROW_Q + t * 16 + h * 8 : s * MSG + ROW_Q + t * 16 + h * 8 + 8, :] for t in range(2)],
-                axis=0,
-            )
-            asked[unit] = asks
-            fresh_rows[unit] = jnp.concatenate(
+            fresh_rows[s * 2 + h] = jnp.concatenate(
                 [rows_old[s * 24 + 16 + h : s * 24 + 17 + h, :]]
-                + [moved[s * MSG + ROW_F + t * 4 + h : s * MSG + ROW_F + t * 4 + h + 1, :] for t in range(2)]
+                + [moved[s * 16 + t * 4 + h : s * 16 + t * 4 + h + 1, :] for t in range(2)]
                 + [rows_old[s * 24 + 18 + h : s * 24 + 19 + h, :]]
-                + [moved[s * MSG + ROW_F + t * 4 + 2 + h : s * MSG + ROW_F + t * 4 + 3 + h, :] for t in range(2)]
+                + [moved[s * 16 + t * 4 + 2 + h : s * 16 + t * 4 + 3 + h, :] for t in range(2)]
                 + [jnp.zeros((2, 128), F32)],
                 axis=0,
             )
-            keys = key_ref[s, :, h * 128 : (h + 1) * 128]
-            values = value_ref[s, :, h * 128 : (h + 1) * 128]
-            scores = (
-                lax.dot_general(asks.astype(BF16), keys, (((1,), (1,)), ((), ())), preferred_element_type=F32) * SCALE
-            )
-            scores = jnp.where(usable, scores, NEGATIVE)
-            top = jnp.max(scores, axis=1, keepdims=True).astype(BF16).astype(F32)
-            weights = jnp.where(usable, jnp.exp(scores - top), 0.0)
-            total = jnp.sum(weights, axis=1, keepdims=True)
-            mixed = jnp.dot(weights.astype(BF16), values, preferred_element_type=F32)
-            high = total.astype(BF16).astype(F32)
-            stats = jnp.where(lanes == 0, top, jnp.where(lanes == 1, high, total - high))
-            part_out[unit] = jnp.concatenate([mixed, stats], axis=0).astype(BF16)
-    part_in[c] = part_out[c]
-    over_ctx(lambda p: send(part_out.at[p], part_in.at[c], 3, {"ctx": p}))
 
     arrived(sel_mp, 2, N_MP - 1)
     total = sel_mp[0]
@@ -303,17 +320,20 @@
         keep = jnp.where(step_of >= u, jnp.exp(recents[u] - overall), 0.0)
         numerator += fresh[3 + u : 4 + u, :] * keep
         denominator += keep
-    done = jnp.concatenate([numerator / denominator, jnp.zeros((8, 128), F32)], axis=0).astype(BF16)
-    fin_out[0] = done
-    fin_in[c] = done
+    done = numerator / denominator
+    fin_out[0] = done[8:24, :].astype(BF16)
+    fin_in[c] = done[8:24, :].astype(BF16)
     over_ctx(lambda p: send(fin_out.at[0], fin_in.at[c], 5, {"ctx": p}))
+    one_out[0] = done[0:8, :]
+    one_in[c] = done[0:8, :]
+    over_ctx(lambda p: send(one_out.at[0], one_in.at[c], 10, {"ctx": p}))
 
     arrived(sel_ctx, 4, N_CTX - 1)
     total = sel_ctx[0]
     for k in range(1, N_CTX):
         total += sel_ctx[k]
     columns = jnp.transpose(total)
-    arrived(size_in, 8, N_DP - 1)
+    arrived(size_in, 9, N_DP - 1)
     for s in range(SLOTS):
         moved_sizes[s * 8 : (s + 1) * 8, :] = size_in[target_group[s]]
     for k in (8, 13, 14):
@@ -359,10 +379,8 @@
     mam_in[d] = mam_message(d)
 
     arrived(fin_in, 5, N_CTX - 1)
-    finished = [fin_in[k].astype(F32) for k in range(N_CTX)]
-    for s in range(SLOTS):
-        for h in range(2):
-            back_rows[s * 32 + h * 16 : s * 32 + h * 16 + 16, :] = finished[s * 2 + h][8:24, :]
+    for k in range(N_CTX):
+        back_rows[k * 16 : k * 16 + 16, :] = fin_in[k].astype(F32)
 
     def ans_message(p):
         total = back_rows[0:32, :] * leaves(0, p)
@@ -376,9 +394,10 @@
 
     over_dp(ans_one)
     ans_in[d] = ans_message(d)
+    arrived(one_in, 10, N_CTX - 1)
     for s in range(SLOTS):
         for h in range(2):
-            rows_old[s * 24 + h * 8 : s * 24 + h * 8 + 8, :] = finished[s * 2 + h][0:8, :]
+            rows_old[s * 24 + h * 8 : s * 24 + h * 8 + 8, :] = one_in[s * 2 + h]
     for j in range(16):
         att_ref[0, :, j * 128 : (j + 1) * 128] = rows_old[pl.ds(j, SLOTS, stride=24), :].astype(BF16)
 
@@ -405,11 +424,13 @@
 
     sent(table_in, 0, N_DP - 1)
     sent(ask_out, 1, N_DP - 1)
-    sent(size_out, 8, N_DP - 1)
+    sent(new_out, 8, N_DP - 1)
+    sent(size_out, 9, N_DP - 1)
     sent(sel_mp, 2, N_MP - 1)
     sent(part_out, 3, N_CTX - 1)
     sent(sel_ctx, 4, N_CTX - 1)
     sent(fin_in, 5, N_CTX - 1)
+    sent(one_in, 10, N_CTX - 1)
     sent(mam_out, 6, N_DP - 1)
     sent(ans_out, 7, N_DP - 1)
 
@@ -451,6 +472,7 @@
         skip_gain.reshape(1, CHAN),
         select_weight,
     )
+    operands = tuple(pltpu.with_memory_space_constraint(x, pltpu.HBM) for x in operands)
     return pl.pallas_call(
         kernel,
         out_shape=(
@@ -468,11 +490,13 @@
             pltpu.VMEM((SLOTS, N_DP, 128), F32),
             pltpu.VMEM((SLOTS * ROWS, 128), F32),
             pltpu.VMEM((SLOTS * 24, 128), F32),
-            pltpu.VMEM((N_DP, MSG, 128), BF16),
-            pltpu.VMEM((N_DP, MSG, 128), BF16),
+            pltpu.VMEM((N_DP, 32, 128), BF16),
+            pltpu.VMEM((N_DP, 32, 128), BF16),
+            pltpu.VMEM((N_DP, 16, 128), BF16),
+            pltpu.VMEM((N_DP, 16, 128), BF16),
             pltpu.VMEM((N_DP, 8, 128), F32),
             pltpu.VMEM((N_DP, 8, 128), F32),
-            pltpu.VMEM((SLOTS * MSG, 128), F32),
+            pltpu.VMEM((SLOTS * 16, 128), F32),
             pltpu.VMEM((SLOTS * 8, 128), F32),
             pltpu.VMEM((8, 24, 128), F32),
             pltpu.VMEM((8, 8, 128), F32),
@@ -483,8 +507,10 @@
             pltpu.VMEM((N_CTX, 8, 128), F32),
             pltpu.VMEM((N_CTX, 48, 128), BF16),
             pltpu.VMEM((N_CTX, 48, 128), BF16),
-            pltpu.VMEM((1, 32, 128), BF16),
-            pltpu.VMEM((N_CTX, 32, 128), BF16),
+            pltpu.VMEM((1, 16, 128), BF16),
+            pltpu.VMEM((N_CTX, 16, 128), BF16),
+            pltpu.VMEM((1, 8, 128), F32),
+            pltpu.VMEM((N_CTX, 8, 128), F32),
             pltpu.VMEM((3, 8, CHAN), F32),
             pltpu.VMEM((SLOTS * 8, 128), F32),
             pltpu.VMEM((N_DP, 8, 128), F32),
@@ -492,11 +518,11 @@
             pltpu.VMEM((N_DP, 32, 128), BF16),
             pltpu.VMEM((N_DP, 32, 128), BF16),
             pltpu.VMEM((SLOTS * 32, 128), F32),
-            pltpu.SemaphoreType.DMA((9,)),
-            pltpu.SemaphoreType.DMA((9,)),
+            pltpu.SemaphoreType.DMA((11,)),
+            pltpu.SemaphoreType.DMA((11,)),
         ],
         compiler_params=pltpu.CompilerParams(
-            collective_id=0, has_side_effects=True, vmem_limit_bytes=60 * 2**20
+            collective_id=0, has_side_effects=True, vmem_limit_bytes=32 * 2**20
         ),
     )(*operands)
 

time: 51.1 us -> 44 us (0.86)
  Pallas kernels: 48.2 us -> 42 us
  local copies, waits for them, and re-layouts: 2.05 us -> 1.22 us
    pallas_call x1, Pallas kernels: 48.2 us -> 42 us  [on_device(): pl.pallas_call(kernel, out_shape=(jax.ShapeDtypeStruct((3, SLOTS, 2048),...]
    unnamed x4 -> x2, local copies, waits for them, and re-layouts: 2.05 us -> 1.22 us
where the time goes in v3:
time: 44 us; the launch traced here: 43.8 us
  Pallas kernels  42 us (95%)
  local copies, waits for them, and re-layouts  1.22 us (3%)
  between operations  0.65 us (1%)
    pallas_call x1, Pallas kernels, on_device(): pl.pallas_call(kernel, out_shape=(jax.ShapeDtypeStruct((3, SLOTS, 2048),...  42 us
    unnamed x2, local copies, waits for them, and re-layouts  1.22 us

profile of v3, /device:TPU:1, one launch (start us, length us, event | category | flops | bytes accessed | tf_op | source)
XLA Modules:
  0.0 43.8 jit_solution(4452293802804531045)
XLA Ops:
  0.6 42.0 %shard_map.167 = (bf16[3,4,2048]{2,1,0:T(4,128)(2,1)S(1)}, bf16[3,4,512]{2,1,0:T(4,128)(2,1)S(1)}) custom-call(s32[4]{0:T(128)} %refs_0_.1, s32[4]{0:T(128)} %refs_1_.1, s32[4]{0:T(128)} %refs_2_.1, bf16[4,256,256]{2,1,0:T(8,128)(2,1)} %refs_3_.1, bf16[4,256,256]{2,1,0:T(8,128)(2,1)} %refs_4_.1, bf16[3,4,2048]{2,1,0:T(4,128)(2,1)} %refs_5_.1, ...), custom_call_target="tpu_custom_call" | custom-call | tf_op jit(solution)/shard_map/pallas_call | solution.py:476
  42.6 0.6 %copy.20 = bf16[3,4,2048]{2,1,0:T(4,128)(2,1)} copy(bf16[3,4,2048]{2,1,0:T(4,128)(2,1)S(1)} %get-tuple-element.4) | data formatting | bytes 98304
  43.2 0.6 %copy.21 = bf16[3,4,512]{2,1,0:T(4,128)(2,1)} copy(bf16[3,4,512]{2,1,0:T(4,128)(2,1)S(1)} %get-tuple-element.5) | data formatting | bytes 24576

commit v4 on v3

v4 whole, which is shorter than its diff:
```python
import functools

import jax
import jax.numpy as jnp
from jax import lax
from jax.experimental import pallas as pl
from jax.experimental.pallas import tpu as pltpu
from jax.sharding import PartitionSpec as P

HEAD = 128
NEGATIVE = -1e30
SCALE = HEAD**-0.5
MESH = pl.DeviceIdType.MESH
F32 = jnp.float32
BF16 = jnp.bfloat16

N_DP = 16
N_CTX = 8
N_MP = 4
SLOTS = 4
UNITS = 8
BLOCK = 256
CHAN = 512
CHUNKS = CHAN // 128

ROW_Q = 0
ROW_M = 32
ROW_S = 40
ROWS = 48

FIRST_LOADS = (1, 2)
LATER_LOADS = (5, 6, 9, 10, 0, 3, 4, 7, 11, 12, 15, 8, 13, 14)

TABLE, ASK, ONE, NEW, PART, SELECT_MP, SELECT_CTX, ONE_DONE, DONE, MAMBA, ANSWER = range(11)


def kernel(*refs):
    operands, (att_ref, mam_ref), rest = refs[:16], refs[16:18], refs[18:]
    local, in_sem, rest = rest[:16], rest[16], rest[17:]
    run(operands, local, in_sem, att_ref, mam_ref, *rest)


def run(
    operands,
    local,
    in_sem,
    att_ref,
    mam_ref,
    table_out,
    table_in,
    member,
    rows_new,
    rows_old,
    ask_out,
    ask_in,
    new_out,
    new_in,
    moved,
    asked_one,
    asked,
    asked_new,
    fresh_one,
    fresh_new,
    mixed_rows,
    stats_rows,
    filt,
    sel_out,
    sel_mp,
    sel_sum,
    sel_ctx,
    one_part_out,
    one_part_in,
    part_out,
    part_in,
    fin_out,
    fin_in,
    one_out,
    one_in,
    scan_rows,
    mam_rows,
    mam_out,
    mam_in,
    ans_out,
    ans_in,
    back_rows,
    all_rows,
    send_sem,
    recv_sem,
):
    (lengths, target_group, target_slot, key_ref, value_ref, query_ref, fresh_ref, recent_ref) = local[:8]
    (state_ref, inputs_ref, steps_ref, taps_ref, bias_ref, decay_ref, skip_ref, select_ref) = local[8:]
    loads = [pltpu.make_async_copy(operands[k], local[k], in_sem.at[k]) for k in range(16)]
    for k in FIRST_LOADS:
        loads[k].start()

    d = lax.axis_index("dp")
    c = lax.axis_index("ctx")
    m = lax.axis_index("mp")

    def far_first(here, count, fn):
        def body(k, carry):
            step = (k + 1) // 2
            p = here + count // 2 + jnp.where(k == 2 * step, step, -step)
            fn(jnp.where(p >= count, p - count, p))
            return carry

        lax.fori_loop(0, count - 1, body, 0)

    def over_dp(fn):
        far_first(d, N_DP, fn)

    def over_ctx(fn):
        far_first(c, N_CTX, fn)

    def over_mp(fn):
        far_first(m, N_MP, fn)

    def send(src, dst, phase, device):
        pltpu.make_async_remote_copy(
            src_ref=src,
            dst_ref=dst,
            send_sem=send_sem.at[phase],
            recv_sem=recv_sem.at[phase],
            device_id=device,
            device_id_type=MESH,
        ).start()

    def arrived(buffer, phase, count):
        part = buffer.at[pl.ds(0, count)]
        pltpu.make_async_copy(part, part, recv_sem.at[phase]).wait()

    def sent(buffer, phase, count):
        part = buffer.at[pl.ds(0, count)]
        pltpu.make_async_copy(part, part, send_sem.at[phase]).wait()

    barrier = pltpu.get_barrier_semaphore()

    def greet(device):
        pl.semaphore_signal(barrier, inc=1, device_id=device, device_id_type=MESH)

    over_dp(lambda p: greet({"dp": p}))
    over_ctx(lambda p: greet({"ctx": p}))
    over_mp(lambda p: greet({"mp": p}))
    for k in LATER_LOADS:
        loads[k].start()

    loads[1].wait()
    loads[2].wait()
    lane = lax.broadcasted_iota(jnp.int32, (1, 128), 1)
    landing = jnp.full((1, 128), -1, jnp.int32)
    for s in range(SLOTS):
        landing = jnp.where(lane == s, target_group[s] * SLOTS + target_slot[s], landing)
    table_out[0] = landing
    table_in[d] = landing
    pl.semaphore_wait(barrier, (N_DP - 1) + (N_CTX - 1) + (N_MP - 1))

    over_dp(lambda p: send(table_out.at[0], table_in.at[d], TABLE, {"dp": p}))

    for k in (5, 6, 9, 10):
        loads[k].wait()
    for t in (1, 2):
        q = query_ref[t].astype(F32)
        for j in range(16):
            rows_new[pl.ds(ROW_Q + j * 2 + t - 1, SLOTS, stride=ROWS), :] = q[:, j * 128 : (j + 1) * 128]
        x = inputs_ref[t, 0].astype(F32)
        for ch in range(CHUNKS):
            rows_new[pl.ds(ROW_M + (t - 1) * 4 + ch, SLOTS, stride=ROWS), :] = x[:, ch * 128 : (ch + 1) * 128]
        x = steps_ref[t]
        for ch in range(CHUNKS):
            rows_new[pl.ds(ROW_S + (t - 1) * 4 + ch, SLOTS, stride=ROWS), :] = x[:, ch * 128 : (ch + 1) * 128]
    q = query_ref[0].astype(F32)
    for j in range(16):
        rows_old[pl.ds(j, SLOTS, stride=24), :] = q[:, j * 128 : (j + 1) * 128]
    for kv in range(2):
        f = fresh_ref[0, kv].astype(F32)
        for h in range(2):
            rows_old[pl.ds(16 + kv * 2 + h, SLOTS, stride=24), :] = f[:, h * 128 : (h + 1) * 128]

    units = [(s, h) for s in range(SLOTS) for h in range(2)]

    def attention(questions, rows):
        positions = lax.broadcasted_iota(jnp.int32, (rows, BLOCK), 1) + c * BLOCK
        lanes = lax.broadcasted_iota(jnp.int32, (rows, 128), 1)
        scores = [
            lax.dot_general(
                questions[k],
                key_ref[s, :, h * 128 : (h + 1) * 128],
                (((1,), (1,)), ((), ())),
                preferred_element_type=F32,
            )
            * SCALE
            for k, (s, h) in enumerate(units)
        ]
        usable = [positions < lengths[s] for s, h in units]
        scores = [jnp.where(usable[k], scores[k], NEGATIVE) for k in range(UNITS)]
        tops = [jnp.max(x, axis=1, keepdims=True).astype(BF16).astype(F32) for x in scores]
        weights = [jnp.where(usable[k], jnp.exp(scores[k] - tops[k]), 0.0) for k in range(UNITS)]
        totals = [jnp.sum(x, axis=1, keepdims=True) for x in weights]
        mixed = [
            jnp.dot(weights[k].astype(BF16), value_ref[s, :, h * 128 : (h + 1) * 128], preferred_element_type=F32)
            for k, (s, h) in enumerate(units)
        ]
        stats = []
        for k in range(UNITS):
            high = totals[k].astype(BF16).astype(F32)
            stats.append(jnp.where(lanes == 0, tops[k], jnp.where(lanes == 1, high, totals[k] - high)))
        return mixed, stats

    for s in range(SLOTS):
        for h in range(2):
            asked_one[s * 2 + h] = rows_old[s * 24 + h * 8 : s * 24 + h * 8 + 8, :]
            fresh_one[s * 2 + h] = jnp.concatenate(
                [
                    rows_old[s * 24 + 16 + h : s * 24 + 17 + h, :],
                    rows_old[s * 24 + 18 + h : s * 24 + 19 + h, :],
                    jnp.zeros((6, 128), F32),
                ],
                axis=0,
            )
    for k in (0, 3, 4):
        loads[k].wait()
    mixed, stats = attention([asked_one[k].astype(BF16) for k in range(UNITS)], 8)
    for k in range(UNITS):
        one_part_out[k] = jnp.concatenate([mixed[k], stats[k]], axis=0).astype(BF16)
    one_part_in[c] = one_part_out[c]
    over_ctx(lambda p: send(one_part_out.at[p], one_part_in.at[c], ONE, {"ctx": p}))

    arrived(table_in, TABLE, N_DP - 1)
    table = table_in[...].reshape(N_DP, 128)
    for i in range(SLOTS):
        hit = jnp.where(table == d * SLOTS + i, 1.0, 0.0).astype(F32)
        member[i] = jnp.broadcast_to(jnp.max(hit, axis=1, keepdims=True), (N_DP, 128))

    def chosen(p, first, last):
        total = rows_new[first:last, :] * member[0, pl.ds(p, 1), :]
        for i in range(1, SLOTS):
            total += rows_new[i * ROWS + first : i * ROWS + last, :] * member[i, pl.ds(p, 1), :]
        return total

    def message(first, last, out, into, phase):
        def one(p):
            out[p] = chosen(p, first, last).astype(out.dtype)
            send(out.at[p], into.at[d], phase, {"dp": p})

        over_dp(one)
        into[d] = chosen(d, first, last).astype(out.dtype)

    message(ROW_Q, ROW_M, ask_out, ask_in, ASK)
    message(ROW_M, ROWS, new_out, new_in, NEW)

    for s in range(SLOTS):
        for k in range(N_CTX):
            asked_new[s * N_CTX + k] = rows_new[s * ROWS + k * 4 : s * ROWS + k * 4 + 4, :]
    for t in (1, 2):
        for kv in range(2):
            f = fresh_ref[t, kv].astype(F32)
            for s in range(SLOTS):
                for h in range(2):
                    fresh_new[s * 2 + h, (t - 1) * 2 + kv : (t - 1) * 2 + kv + 1, :] = f[s : s + 1, h * 128 : (h + 1) * 128]
    kv_head = c // (N_CTX // 2)

    def pair_rows(ref, row):
        return jnp.concatenate(
            [jnp.broadcast_to(ref[s * 2 + kv_head, row : row + 1, :], (4, 128)) for s in range(SLOTS)], axis=0
        )

    def head_rows(ref):
        return jnp.concatenate([ref[s * N_CTX + c] for s in range(SLOTS)], axis=0)

    def score_of(questions, keys):
        return jnp.sum(questions * keys, axis=1, keepdims=True) * SCALE

    own_asks = head_rows(asked_new)
    last_step = lax.broadcasted_iota(jnp.int32, (16, 1), 0) % 2 == 1
    second_score = score_of(own_asks, pair_rows(fresh_new, 0))
    third_score = jnp.where(last_step, score_of(own_asks, pair_rows(fresh_new, 2)), NEGATIVE)
    second_value = pair_rows(fresh_new, 1)
    third_value = pair_rows(fresh_new, 3)

    for k in (7, 11, 12, 15):
        loads[k].wait()
    taps = taps_ref[...].astype(F32)
    bias = bias_ref[...]
    window = [recent_ref[k].astype(F32) for k in range(3)] + [inputs_ref[0, 0].astype(F32)]

    def filtered(parts):
        total = parts[0] * taps[0:1, :]
        for k in range(1, 4):
            total += parts[k] * taps[k : k + 1, :]
        total += bias
        return (total * jax.nn.sigmoid(total)).astype(BF16).astype(F32)

    filt[0, 0:SLOTS, :] = filtered(window)
    weight = select_ref[...]
    weight = jnp.concatenate([weight] * SLOTS, axis=0)

    arrived(ask_in, ASK, N_DP - 1)
    questions = []
    for s in range(SLOTS):
        queries = ask_in[target_group[s]]
        questions += [queries[0:16, :], queries[16:32, :]]
        queries = queries.astype(F32)
        for k in range(N_CTX):
            asked[s * N_CTX + k] = queries[k * 4 : k * 4 + 4, :]
    mixed, stats = attention(questions, 16)
    for k in range(UNITS):
        for j in range(4):
            at = ((k % 2) * 4 + j) * 16 + (k // 2) * 4
            mixed_rows[at : at + 4, :] = mixed[k][j * 4 : j * 4 + 4, :]
            stats_rows[at : at + 4, :] = stats[k][j * 4 : j * 4 + 4, :]
    for k in range(N_CTX):
        part_out[k] = jnp.concatenate(
            [mixed_rows[k * 16 : k * 16 + 16, :], stats_rows[k * 16 : k * 16 + 16, :]], axis=0
        ).astype(BF16)
    part_in[c] = part_out[c]
    over_ctx(lambda p: send(part_out.at[p], part_in.at[c], PART, {"ctx": p}))

    arrived(new_in, NEW, N_DP - 1)
    for s in range(SLOTS):
        moved[s * 16 : s * 16 + 16, :] = new_in[target_group[s]].astype(F32)

    def lined_up(ref, row, stride):
        return jnp.concatenate([ref[pl.ds(row + ch, SLOTS, stride=stride), :] for ch in range(CHUNKS)], axis=1)

    for t in (1, 2):
        window = window[1:] + [lined_up(moved, (t - 1) * 4, 16)]
        filt[t, 0:SLOTS, :] = filtered(window)
    own = lax.broadcasted_iota(jnp.int32, (8, 128), 1) // 32 == lax.broadcasted_iota(jnp.int32, (8, 128), 0)
    picks = []
    for t in range(3):
        product = lax.dot_general(
            filt[t].astype(BF16), weight, (((1,), (1,)), ((), ())), preferred_element_type=F32
        )
        picks.append(jnp.sum(jnp.where(own, product, 0.0), axis=0, keepdims=True))
    sel_out[0] = jnp.concatenate(picks + [jnp.zeros((5, 128), F32)], axis=0)
    sel_mp[m] = sel_out[0]
    over_mp(lambda p: send(sel_out.at[0], sel_mp.at[m], SELECT_MP, {"mp": p}))

    def finish(part_in, rows, score, value):
        parts = [part_in[k].astype(F32) for k in range(N_CTX)]
        tops = [part[rows : 2 * rows, 0:1] for part in parts]
        overall = score
        for k in range(N_CTX):
            overall = jnp.maximum(overall, tops[k])
        denominator = jnp.exp(score - overall)
        numerator = value * denominator
        for k in range(N_CTX):
            keep = jnp.exp(tops[k] - overall)
            numerator += parts[k][0:rows, :] * keep
            denominator += (parts[k][rows : 2 * rows, 1:2] + parts[k][rows : 2 * rows, 2:3]) * keep
        return numerator / denominator, overall, denominator

    own_pair = fresh_one[c]
    arrived(one_part_in, ONE, N_CTX - 1)
    one_out[0] = finish(one_part_in, 8, score_of(asked_one[c], own_pair[0:1, :]), own_pair[1:2, :])[0]
    one_in[c] = one_out[0]
    over_ctx(lambda p: send(one_out.at[0], one_in.at[c], ONE_DONE, {"ctx": p}))

    arrived(sel_mp, SELECT_MP, N_MP - 1)
    total = sel_mp[0]
    for k in range(1, N_MP):
        total += sel_mp[k]
    sel_sum[0] = total
    sel_ctx[c] = total
    over_ctx(lambda p: send(sel_sum.at[0], sel_ctx.at[c], SELECT_CTX, {"ctx": p}))

    def leaves(s, p):
        return jnp.where(target_group[s] == p, 1.0, 0.0).astype(F32)

    def returned(rows, p):
        total = rows[0:8, :] * leaves(0, p)
        for s in range(1, SLOTS):
            total += rows[s * 8 : (s + 1) * 8, :] * leaves(s, p)
        return total

    first_score = score_of(head_rows(asked), pair_rows(fresh_one, 0))
    first_value = pair_rows(fresh_one, 1)
    arrived(part_in, PART, N_CTX - 1)
    done, overall, denominator = finish(part_in, 16, first_score, first_value)
    weight_log = jnp.broadcast_to(overall + jnp.log(denominator), (16, 128))
    for s in range(SLOTS):
        back_rows[s * 8 : s * 8 + 4, :] = done[s * 4 : s * 4 + 4, :]
        back_rows[s * 8 + 4 : s * 8 + 8, :] = weight_log[s * 4 : s * 4 + 4, :]

    def ans_one(p):
        ans_out[p] = returned(back_rows, p)
        send(ans_out.at[p], ans_in.at[d], ANSWER, {"dp": p})

    over_dp(ans_one)
    ans_in[d] = returned(back_rows, d)

    for k in (8, 13, 14):
        loads[k].wait()
    rates = jnp.exp(decay_ref[...])
    sizes = [steps_ref[0]] + [lined_up(moved, 8 + (t - 1) * 4, 16) for t in (1, 2)]
    inputs = [filt[t, 0:SLOTS, :] for t in range(3)]

    def gated(result, t):
        gate = inputs_ref[t, 1].astype(F32)
        return (result * (gate * jax.nn.sigmoid(gate))).astype(BF16)

    arrived(sel_ctx, SELECT_CTX, N_CTX - 1)
    total = sel_ctx[0]
    for k in range(1, N_CTX):
        total += sel_ctx[k]
    columns = jnp.transpose(total)
    for s in range(SLOTS):
        hidden = state_ref[s]
        for t in range(3):
            size = sizes[t][s : s + 1, :]
            into = columns[s * 32 : s * 32 + 16, t : t + 1]
            out = columns[s * 32 + 16 : s * 32 + 32, t : t + 1]
            hidden = jnp.exp(-size * rates) * hidden + into * (size * inputs[t][s : s + 1, :])
            scan_rows[t, s : s + 1, :] = jnp.sum(out * hidden, axis=0, keepdims=True)
    for t in range(3):
        result = scan_rows[t, 0:SLOTS, :] + skip_ref[...] * inputs[t]
        if t == 0:
            mam_ref[0] = gated(result, 0)
        else:
            for ch in range(CHUNKS):
                mam_rows[pl.ds((t - 1) * 4 + ch, SLOTS, stride=8), :] = result[:, ch * 128 : (ch + 1) * 128]

    def mam_one(p):
        mam_out[p] = returned(mam_rows, p)
        send(mam_out.at[p], mam_in.at[d], MAMBA, {"dp": p})

    over_dp(mam_one)
    mam_in[d] = returned(mam_rows, d)

    def picked(ref, i):
        total = ref[0] * member[i, 0:1, :]
        for g in range(1, N_DP):
            total += ref[g] * member[i, g : g + 1, :]
        return total

    arrived(ans_in, ANSWER, N_DP - 1)
    found = [picked(ans_in, i) for i in range(SLOTS)]
    cached = jnp.concatenate([x[0:4, :] for x in found], axis=0)
    cached_log = jnp.concatenate([x[4:8, :] for x in found], axis=0)[:, 0:1]
    overall = jnp.maximum(cached_log, jnp.maximum(second_score, third_score))
    keeps = [jnp.exp(cached_log - overall), jnp.exp(second_score - overall)]
    keeps.append(jnp.where(last_step, jnp.exp(third_score - overall), 0.0))
    done = (cached * keeps[0] + second_value * keeps[1] + third_value * keeps[2]) / (keeps[0] + keeps[1] + keeps[2])
    fin_out[0] = done.astype(BF16)
    fin_in[c] = done.astype(BF16)
    over_ctx(lambda p: send(fin_out.at[0], fin_in.at[c], DONE, {"ctx": p}))

    arrived(one_in, ONE_DONE, N_CTX - 1)
    for s in range(SLOTS):
        for h in range(2):
            rows_old[s * 24 + h * 8 : s * 24 + h * 8 + 8, :] = one_in[s * 2 + h]
    for j in range(16):
        att_ref[0, :, j * 128 : (j + 1) * 128] = rows_old[pl.ds(j, SLOTS, stride=24), :].astype(BF16)

    arrived(mam_in, MAMBA, N_DP - 1)
    for i in range(SLOTS):
        mam_rows[i * 8 : (i + 1) * 8, :] = picked(mam_in, i)
    for t in (1, 2):
        mam_ref[t] = gated(lined_up(mam_rows, (t - 1) * 4, 8), t)

    sent(table_in, TABLE, N_DP - 1)
    sent(ask_out, ASK, N_DP - 1)
    sent(new_out, NEW, N_DP - 1)
    sent(one_part_out, ONE, N_CTX - 1)
    sent(sel_mp, SELECT_MP, N_MP - 1)
    sent(sel_ctx, SELECT_CTX, N_CTX - 1)
    sent(part_out, PART, N_CTX - 1)
    sent(ans_out, ANSWER, N_DP - 1)
    sent(one_in, ONE_DONE, N_CTX - 1)
    sent(mam_out, MAMBA, N_DP - 1)

    arrived(fin_in, DONE, N_CTX - 1)
    for k in range(N_CTX):
        all_rows[k * 16 : (k + 1) * 16, :] = fin_in[k].astype(F32)
    for t in (1, 2):
        for j in range(16):
            att_ref[t, :, j * 128 : (j + 1) * 128] = all_rows[
                pl.ds((j // 2) * 16 + (j % 2) * 2 + t - 1, SLOTS, stride=4), :
            ].astype(BF16)
    sent(fin_in, DONE, N_CTX - 1)


def on_device(
    key_cache,
    value_cache,
    lengths,
    queries,
    fresh_pairs,
    recent_inputs,
    scan_state,
    mamba_inputs,
    step_sizes,
    filter_taps,
    filter_bias,
    decay_logs,
    skip_gain,
    select_weight,
    target_group,
    target_slot,
):
    vmem = pl.BlockSpec(memory_space=pltpu.VMEM)
    operands = (
        lengths,
        target_group,
        target_slot,
        key_cache,
        value_cache,
        queries,
        fresh_pairs,
        jnp.swapaxes(recent_inputs, 0, 1),
        scan_state,
        mamba_inputs,
        step_sizes,
        filter_taps,
        filter_bias.reshape(1, CHAN),
        decay_logs,
        skip_gain.reshape(1, CHAN),
        select_weight,
    )
    operands = tuple(pltpu.with_memory_space_constraint(x, pltpu.HBM) for x in operands)
    return pl.pallas_call(
        kernel,
        out_shape=(
            jax.ShapeDtypeStruct((3, SLOTS, 2048), BF16),
            jax.ShapeDtypeStruct((3, SLOTS, CHAN), BF16),
        ),
        in_specs=[pl.BlockSpec(memory_space=pltpu.HBM)] * 16,
        out_specs=(vmem, vmem),
        scratch_shapes=[pltpu.SMEM((SLOTS,), jnp.int32)] * 3
        + [pltpu.VMEM(x.shape, x.dtype) for x in operands[3:]]
        + [
            pltpu.SemaphoreType.DMA((16,)),
            pltpu.VMEM((1, 1, 128), jnp.int32),
            pltpu.VMEM((N_DP, 1, 128), jnp.int32),
            pltpu.VMEM((SLOTS, N_DP, 128), F32),
            pltpu.VMEM((SLOTS * ROWS, 128), F32),
            pltpu.VMEM((SLOTS * 24, 128), F32),
            pltpu.VMEM((N_DP, 32, 128), BF16),
            pltpu.VMEM((N_DP, 32, 128), BF16),
            pltpu.VMEM((N_DP, 16, 128), BF16),
            pltpu.VMEM((N_DP, 16, 128), BF16),
            pltpu.VMEM((SLOTS * 16, 128), F32),
            pltpu.VMEM((UNITS, 8, 128), F32),
            pltpu.VMEM((SLOTS * N_CTX, 4, 128), F32),
            pltpu.VMEM((SLOTS * N_CTX, 4, 128), F32),
            pltpu.VMEM((UNITS, 8, 128), F32),
            pltpu.VMEM((UNITS, 8, 128), F32),
            pltpu.VMEM((N_CTX * 16, 128), F32),
            pltpu.VMEM((N_CTX * 16, 128), F32),
            pltpu.VMEM((3, 8, CHAN), F32),
            pltpu.VMEM((1, 8, 128), F32),
            pltpu.VMEM((N_MP, 8, 128), F32),
            pltpu.VMEM((1, 8, 128), F32),
            pltpu.VMEM((N_CTX, 8, 128), F32),
            pltpu.VMEM((N_CTX, 16, 128), BF16),
            pltpu.VMEM((N_CTX, 16, 128), BF16),
            pltpu.VMEM((N_CTX, 32, 128), BF16),
            pltpu.VMEM((N_CTX, 32, 128), BF16),
            pltpu.VMEM((1, 16, 128), BF16),
            pltpu.VMEM((N_CTX, 16, 128), BF16),
            pltpu.VMEM((1, 8, 128), F32),
            pltpu.VMEM((N_CTX, 8, 128), F32),
            pltpu.VMEM((3, 8, CHAN), F32),
            pltpu.VMEM((SLOTS * 8, 128), F32),
            pltpu.VMEM((N_DP, 8, 128), F32),
            pltpu.VMEM((N_DP, 8, 128), F32),
            pltpu.VMEM((N_DP, 8, 128), F32),
            pltpu.VMEM((N_DP, 8, 128), F32),
            pltpu.VMEM((SLOTS * 8, 128), F32),
            pltpu.VMEM((N_CTX * 16, 128), F32),
            pltpu.SemaphoreType.DMA((11,)),
            pltpu.SemaphoreType.DMA((11,)),
        ],
        compiler_params=pltpu.CompilerParams(
            collective_id=0, has_side_effects=True, vmem_limit_bytes=32 * 2**20
        ),
    )(*operands)


def solution(mesh):
    placed = (
        P("dp", "ctx", "mp"),
        P("dp", "ctx", "mp"),
        P("dp"),
        P(None, "dp", "mp"),
        P(None, None, "dp", "mp"),
        P("dp", None, ("ctx", "mp")),
        P("dp", None, ("ctx", "mp")),
        P(None, None, "dp", ("ctx", "mp")),
        P(None, "dp", ("ctx", "mp")),
        P(None, ("ctx", "mp")),
        P(("ctx", "mp")),
        P(None, ("ctx", "mp")),
        P(("ctx", "mp")),
        P(None, ("ctx", "mp")),
        P("dp"),
        P("dp"),
    )
    return jax.shard_map(
        on_device,
        mesh=mesh,
        in_specs=placed,
        out_specs=(P(None, "dp", "mp"), P(None, "dp", ("ctx", "mp"))),
        check_vma=False,
    )
```

time: 44 us -> 42.7 us (0.970)
  Pallas kernels: 42 us -> 40.7 us
    pallas_call x1, Pallas kernels: 42 us -> 40.7 us  [on_device(): pl.pallas_call(kernel, out_shape=(jax.ShapeDtypeStruct((3, SLOTS, 2048),...]
where the time goes in v4:
time: 42.7 us; the launch traced here: 42.6 us
  Pallas kernels  40.7 us (95%)
  local copies, waits for them, and re-layouts  1.22 us (3%)
  between operations  0.65 us (2%)
    pallas_call x1, Pallas kernels, on_device(): pl.pallas_call(kernel, out_shape=(jax.ShapeDtypeStruct((3, SLOTS, 2048),...  40.7 us
    unnamed x2, local copies, waits for them, and re-layouts  1.22 us

profile of v4, /device:TPU:1, one launch (start us, length us, event | category | flops | bytes accessed | tf_op | source)
XLA Modules:
  0.0 42.6 jit_solution(13635280335327013283)
XLA Ops:
  0.6 40.7 %shard_map.167 = (bf16[3,4,2048]{2,1,0:T(4,128)(2,1)S(1)}, bf16[3,4,512]{2,1,0:T(4,128)(2,1)S(1)}) custom-call(s32[4]{0:T(128)} %refs_0_.1, s32[4]{0:T(128)} %refs_1_.1, s32[4]{0:T(128)} %refs_2_.1, bf16[4,256,256]{2,1,0:T(8,128)(2,1)} %refs_3_.1, bf16[4,256,256]{2,1,0:T(8,128)(2,1)} %refs_4_.1, bf16[3,4,2048]{2,1,0:T(4,128)(2,1)} %refs_5_.1, ...), custom_call_target="tpu_custom_call" | custom-call | tf_op jit(solution)/shard_map/pallas_call | solution.py:521
  41.3 0.6 %copy.20 = bf16[3,4,2048]{2,1,0:T(4,128)(2,1)} copy(bf16[3,4,2048]{2,1,0:T(4,128)(2,1)S(1)} %get-tuple-element.4) | data formatting | bytes 98304
  42.0 0.6 %copy.21 = bf16[3,4,512]{2,1,0:T(4,128)(2,1)} copy(bf16[3,4,512]{2,1,0:T(4,128)(2,1)S(1)} %get-tuple-element.5) | data formatting | bytes 24576

commit v5 on v4

--- a/solution.py
+++ b/solution.py
@@ -17,21 +17,21 @@
 N_DP = 16
 N_CTX = 8
 N_MP = 4
+N_SEL = N_CTX * N_MP
 SLOTS = 4
 UNITS = 8
 BLOCK = 256
 CHAN = 512
 CHUNKS = CHAN // 128
 
-ROW_Q = 0
-ROW_M = 32
-ROW_S = 40
-ROWS = 48
-
-FIRST_LOADS = (1, 2)
-LATER_LOADS = (5, 6, 9, 10, 0, 3, 4, 7, 11, 12, 15, 8, 13, 14)
-
-TABLE, ASK, ONE, NEW, PART, SELECT_MP, SELECT_CTX, ONE_DONE, DONE, MAMBA, ANSWER = range(11)
+ROW_M = 0
+ROW_S = 8
+ROWS = 16
+
+FIRST_LOADS = (1, 2, 5)
+LATER_LOADS = (6, 9, 10, 0, 3, 4, 7, 11, 12, 15, 8, 13, 14)
+
+TABLE, ASK, ONE, NEW, PART, SELECT, ONE_DONE, DONE, MAMBA, ANSWER, FORWARD = range(11)
 
 
 def kernel(*refs):
@@ -49,6 +49,7 @@
     table_out,
     table_in,
     member,
+    rows_ask,
     rows_new,
     rows_old,
     ask_out,
@@ -65,9 +66,7 @@
     stats_rows,
     filt,
     sel_out,
-    sel_mp,
-    sel_sum,
-    sel_ctx,
+    sel_in,
     one_part_out,
     one_part_in,
     part_out,
@@ -76,6 +75,8 @@
     fin_in,
     one_out,
     one_in,
+    decays,
+    pushed,
     scan_rows,
     mam_rows,
     mam_out,
@@ -86,6 +87,7 @@
     all_rows,
     send_sem,
     recv_sem,
+    ask_sem,
 ):
     (lengths, target_group, target_slot, key_ref, value_ref, query_ref, fresh_ref, recent_ref) = local[:8]
     (state_ref, inputs_ref, steps_ref, taps_ref, bias_ref, decay_ref, skip_ref, select_ref) = local[8:]
@@ -96,6 +98,8 @@
     d = lax.axis_index("dp")
     c = lax.axis_index("ctx")
     m = lax.axis_index("mp")
+    me = c * N_MP + m
+    partner = d + 1 - 2 * (d % 2)
 
     def far_first(here, count, fn):
         def body(k, carry):
@@ -106,6 +110,13 @@
 
         lax.fori_loop(0, count - 1, body, 0)
 
+    def first_started(here, count, fn):
+        def body(k, carry):
+            fn(k + jnp.where(k >= here, 1, 0))
+            return carry
+
+        lax.fori_loop(0, count - 1, body, 0)
+
     def over_dp(fn):
         far_first(d, N_DP, fn)
 
@@ -114,6 +125,9 @@
 
     def over_mp(fn):
         far_first(m, N_MP, fn)
+
+    def over_sel(fn):
+        far_first(me, N_SEL, lambda p: fn({"ctx": p // N_MP, "mp": p % N_MP}))
 
     def send(src, dst, phase, device):
         pltpu.make_async_remote_copy(
@@ -152,16 +166,37 @@
         landing = jnp.where(lane == s, target_group[s] * SLOTS + target_slot[s], landing)
     table_out[0] = landing
     table_in[d] = landing
-    pl.semaphore_wait(barrier, (N_DP - 1) + (N_CTX - 1) + (N_MP - 1))
-
-    over_dp(lambda p: send(table_out.at[0], table_in.at[d], TABLE, {"dp": p}))
-
-    for k in (5, 6, 9, 10):
-        loads[k].wait()
+    loads[5].wait()
     for t in (1, 2):
         q = query_ref[t].astype(F32)
         for j in range(16):
-            rows_new[pl.ds(ROW_Q + j * 2 + t - 1, SLOTS, stride=ROWS), :] = q[:, j * 128 : (j + 1) * 128]
+            rows_ask[pl.ds(j * 2 + t - 1, SLOTS, stride=32), :] = q[:, j * 128 : (j + 1) * 128]
+    for s in range(SLOTS):
+        ask_out[s] = rows_ask[s * 32 : s * 32 + 32, :].astype(BF16)
+        ask_in[d, s] = ask_out[s]
+    pl.semaphore_wait(barrier, (N_DP - 1) + (N_CTX - 1) + (N_MP - 1))
+
+    over_dp(lambda p: send(table_out.at[0], table_in.at[d], TABLE, {"dp": p}))
+
+    def ask_one(k, carry):
+        step = (k + 1) // 2
+        p = d + N_DP // 2 + 2 * jnp.where(k == 2 * step, step, -step)
+        pltpu.make_async_remote_copy(
+            src_ref=ask_out,
+            dst_ref=ask_in.at[d],
+            send_sem=send_sem.at[ASK],
+            recv_sem=ask_sem.at[d // 2],
+            device_id={"dp": jnp.where(p >= N_DP, p - N_DP, p)},
+            device_id_type=MESH,
+        ).start()
+        return carry
+
+    lax.fori_loop(0, N_DP // 2 - 1, ask_one, 0)
+    send(ask_out, ask_in.at[d], FORWARD, {"dp": partner})
+
+    for k in (6, 9, 10):
+        loads[k].wait()
+    for t in (1, 2):
         x = inputs_ref[t, 0].astype(F32)
         for ch in range(CHUNKS):
             rows_new[pl.ds(ROW_M + (t - 1) * 4 + ch, SLOTS, stride=ROWS), :] = x[:, ch * 128 : (ch + 1) * 128]
@@ -245,12 +280,22 @@
         over_dp(one)
         into[d] = chosen(d, first, last).astype(out.dtype)
 
-    message(ROW_Q, ROW_M, ask_out, ask_in, ASK)
     message(ROW_M, ROWS, new_out, new_in, NEW)
 
+    def forward(k, carry):
+        step = k // 2 + 1
+        p = d + 2 * jnp.where(k == 2 * step - 2, step, N_DP // 2 - step)
+        group = jnp.where(p >= N_DP, p - N_DP, p)
+        block = ask_in.at[group]
+        pltpu.make_async_copy(block, block, ask_sem.at[group // 2]).wait()
+        send(block, block, FORWARD, {"dp": partner})
+        return carry
+
+    lax.fori_loop(0, N_DP // 2 - 1, forward, 0)
+
     for s in range(SLOTS):
         for k in range(N_CTX):
-            asked_new[s * N_CTX + k] = rows_new[s * ROWS + k * 4 : s * ROWS + k * 4 + 4, :]
+            asked_new[s * N_CTX + k] = rows_ask[s * 32 + k * 4 : s * 32 + k * 4 + 4, :]
     for t in (1, 2):
         for kv in range(2):
             f = fresh_ref[t, kv].astype(F32)
@@ -277,7 +322,7 @@
     second_value = pair_rows(fresh_new, 1)
     third_value = pair_rows(fresh_new, 3)
 
-    for k in (7, 11, 12, 15):
+    for k in (7, 8, 11, 12, 13, 14, 15):
         loads[k].wait()
     taps = taps_ref[...].astype(F32)
     bias = bias_ref[...]
@@ -294,14 +339,11 @@
     weight = select_ref[...]
     weight = jnp.concatenate([weight] * SLOTS, axis=0)
 
-    arrived(ask_in, ASK, N_DP - 1)
+    arrived(ask_in, FORWARD, N_DP // 2)
     questions = []
     for s in range(SLOTS):
-        queries = ask_in[target_group[s]]
+        queries = ask_in[target_group[s], target_slot[s]]
         questions += [queries[0:16, :], queries[16:32, :]]
-        queries = queries.astype(F32)
-        for k in range(N_CTX):
-            asked[s * N_CTX + k] = queries[k * 4 : k * 4 + 4, :]
     mixed, stats = attention(questions, 16)
     for k in range(UNITS):
         for j in range(4):
@@ -314,6 +356,10 @@
         ).astype(BF16)
     part_in[c] = part_out[c]
     over_ctx(lambda p: send(part_out.at[p], part_in.at[c], PART, {"ctx": p}))
+    for s in range(SLOTS):
+        queries = ask_in[target_group[s], target_slot[s]].astype(F32)
+        for k in range(N_CTX):
+            asked[s * N_CTX + k] = queries[k * 4 : k * 4 + 4, :]
 
     arrived(new_in, NEW, N_DP - 1)
     for s in range(SLOTS):
@@ -332,9 +378,10 @@
             filt[t].astype(BF16), weight, (((1,), (1,)), ((), ())), preferred_element_type=F32
         )
         picks.append(jnp.sum(jnp.where(own, product, 0.0), axis=0, keepdims=True))
+    arrived(one_part_in, ONE, N_CTX - 1)
     sel_out[0] = jnp.concatenate(picks + [jnp.zeros((5, 128), F32)], axis=0)
-    sel_mp[m] = sel_out[0]
-    over_mp(lambda p: send(sel_out.at[0], sel_mp.at[m], SELECT_MP, {"mp": p}))
+    sel_in[me] = sel_out[0]
+    over_sel(lambda device: send(sel_out.at[0], sel_in.at[me], SELECT, device))
 
     def finish(part_in, rows, score, value):
         parts = [part_in[k].astype(F32) for k in range(N_CTX)]
@@ -351,18 +398,17 @@
         return numerator / denominator, overall, denominator
 
     own_pair = fresh_one[c]
-    arrived(one_part_in, ONE, N_CTX - 1)
     one_out[0] = finish(one_part_in, 8, score_of(asked_one[c], own_pair[0:1, :]), own_pair[1:2, :])[0]
     one_in[c] = one_out[0]
     over_ctx(lambda p: send(one_out.at[0], one_in.at[c], ONE_DONE, {"ctx": p}))
 
-    arrived(sel_mp, SELECT_MP, N_MP - 1)
-    total = sel_mp[0]
-    for k in range(1, N_MP):
-        total += sel_mp[k]
-    sel_sum[0] = total
-    sel_ctx[c] = total
-    over_ctx(lambda p: send(sel_sum.at[0], sel_ctx.at[c], SELECT_CTX, {"ctx": p}))
+    rates = jnp.exp(decay_ref[...])
+    inputs = [filt[t, 0:SLOTS, :] for t in range(3)]
+    for t in range(3):
+        sizes = steps_ref[0] if t == 0 else lined_up(moved, 8 + (t - 1) * 4, 16)
+        pushed[t, 0:SLOTS, :] = sizes * inputs[t]
+        for s in range(SLOTS):
+            decays[t, s] = jnp.exp(-sizes[s : s + 1, :] * rates)
 
     def leaves(s, p):
         return jnp.where(target_group[s] == p, 1.0, 0.0).astype(F32)
@@ -386,31 +432,24 @@
         ans_out[p] = returned(back_rows, p)
         send(ans_out.at[p], ans_in.at[d], ANSWER, {"dp": p})
 
-    over_dp(ans_one)
+    first_started(d, N_DP, ans_one)
     ans_in[d] = returned(back_rows, d)
-
-    for k in (8, 13, 14):
-        loads[k].wait()
-    rates = jnp.exp(decay_ref[...])
-    sizes = [steps_ref[0]] + [lined_up(moved, 8 + (t - 1) * 4, 16) for t in (1, 2)]
-    inputs = [filt[t, 0:SLOTS, :] for t in range(3)]
 
     def gated(result, t):
         gate = inputs_ref[t, 1].astype(F32)
         return (result * (gate * jax.nn.sigmoid(gate))).astype(BF16)
 
-    arrived(sel_ctx, SELECT_CTX, N_CTX - 1)
-    total = sel_ctx[0]
-    for k in range(1, N_CTX):
-        total += sel_ctx[k]
+    arrived(sel_in, SELECT, N_SEL - 1)
+    total = sel_in[0]
+    for k in range(1, N_SEL):
+        total += sel_in[k]
     columns = jnp.transpose(total)
     for s in range(SLOTS):
         hidden = state_ref[s]
         for t in range(3):
-            size = sizes[t][s : s + 1, :]
             into = columns[s * 32 : s * 32 + 16, t : t + 1]
             out = columns[s * 32 + 16 : s * 32 + 32, t : t + 1]
-            hidden = jnp.exp(-size * rates) * hidden + into * (size * inputs[t][s : s + 1, :])
+            hidden = decays[t, s] * hidden + into * pushed[t, s : s + 1, :]
             scan_rows[t, s : s + 1, :] = jnp.sum(out * hidden, axis=0, keepdims=True)
     for t in range(3):
         result = scan_rows[t, 0:SLOTS, :] + skip_ref[...] * inputs[t]
@@ -424,7 +463,7 @@
         mam_out[p] = returned(mam_rows, p)
         send(mam_out.at[p], mam_in.at[d], MAMBA, {"dp": p})
 
-    over_dp(mam_one)
+    first_started(d, N_DP, mam_one)
     mam_in[d] = returned(mam_rows, d)
 
     def picked(ref, i):
@@ -459,11 +498,11 @@
         mam_ref[t] = gated(lined_up(mam_rows, (t - 1) * 4, 8), t)
 
     sent(table_in, TABLE, N_DP - 1)
-    sent(ask_out, ASK, N_DP - 1)
+    sent(ask_in, ASK, N_DP // 2 - 1)
+    sent(ask_in, FORWARD, N_DP // 2)
     sent(new_out, NEW, N_DP - 1)
     sent(one_part_out, ONE, N_CTX - 1)
-    sent(sel_mp, SELECT_MP, N_MP - 1)
-    sent(sel_ctx, SELECT_CTX, N_CTX - 1)
+    sent(sel_in, SELECT, N_SEL - 1)
     sent(part_out, PART, N_CTX - 1)
     sent(ans_out, ANSWER, N_DP - 1)
     sent(one_in, ONE_DONE, N_CTX - 1)
@@ -533,10 +572,11 @@
             pltpu.VMEM((1, 1, 128), jnp.int32),
             pltpu.VMEM((N_DP, 1, 128), jnp.int32),
             pltpu.VMEM((SLOTS, N_DP, 128), F32),
+            pltpu.VMEM((SLOTS * 32, 128), F32),
             pltpu.VMEM((SLOTS * ROWS, 128), F32),
             pltpu.VMEM((SLOTS * 24, 128), F32),
-            pltpu.VMEM((N_DP, 32, 128), BF16),
-            pltpu.VMEM((N_DP, 32, 128), BF16),
+            pltpu.VMEM((SLOTS, 32, 128), BF16),
+            pltpu.VMEM((N_DP, SLOTS, 32, 128), BF16),
             pltpu.VMEM((N_DP, 16, 128), BF16),
             pltpu.VMEM((N_DP, 16, 128), BF16),
             pltpu.VMEM((SLOTS * 16, 128), F32),
@@ -549,9 +589,7 @@
             pltpu.VMEM((N_CTX * 16, 128), F32),
             pltpu.VMEM((3, 8, CHAN), F32),
             pltpu.VMEM((1, 8, 128), F32),
-            pltpu.VMEM((N_MP, 8, 128), F32),
-            pltpu.VMEM((1, 8, 128), F32),
-            pltpu.VMEM((N_CTX, 8, 128), F32),
+            pltpu.VMEM((N_SEL, 8, 128), F32),
             pltpu.VMEM((N_CTX, 16, 128), BF16),
             pltpu.VMEM((N_CTX, 16, 128), BF16),
             pltpu.VMEM((N_CTX, 32, 128), BF16),
@@ -560,6 +598,8 @@
             pltpu.VMEM((N_CTX, 16, 128), BF16),
             pltpu.VMEM((1, 8, 128), F32),
             pltpu.VMEM((N_CTX, 8, 128), F32),
+            pltpu.VMEM((3, SLOTS, 16, CHAN), F32),
+            pltpu.VMEM((3, 8, CHAN), F32),
             pltpu.VMEM((3, 8, CHAN), F32),
             pltpu.VMEM((SLOTS * 8, 128), F32),
             pltpu.VMEM((N_DP, 8, 128), F32),
@@ -570,6 +610,7 @@
             pltpu.VMEM((N_CTX * 16, 128), F32),
             pltpu.SemaphoreType.DMA((11,)),
             pltpu.SemaphoreType.DMA((11,)),
+            pltpu.SemaphoreType.DMA((N_DP // 2,)),
         ],
         compiler_params=pltpu.CompilerParams(
             collective_id=0, has_side_effects=True, vmem_limit_bytes=32 * 2**20

time: 42.7 us -> 41.5 us (0.972)
  Pallas kernels: 40.7 us -> 39.5 us
    pallas_call x1, Pallas kernels: 40.7 us -> 39.5 us  [on_device(): pl.pallas_call(kernel, out_shape=(jax.ShapeDtypeStruct((3, SLOTS, 2048),...]
where the time goes in v5:
time: 41.5 us; the launch traced here: 41.3 us
  Pallas kernels  39.5 us (95%)
  local copies, waits for them, and re-layouts  1.22 us (3%)
  between operations  0.65 us (2%)
    pallas_call x1, Pallas kernels, on_device(): pl.pallas_call(kernel, out_shape=(jax.ShapeDtypeStruct((3, SLOTS, 2048),...  39.5 us
    unnamed x2, local copies, waits for them, and re-layouts  1.22 us

profile of v5, /device:TPU:1, one launch (start us, length us, event | category | flops | bytes accessed | tf_op | source)
XLA Modules:
  0.0 41.3 jit_solution(10906286821599871696)
XLA Ops:
  0.6 39.5 %shard_map.167 = (bf16[3,4,2048]{2,1,0:T(4,128)(2,1)S(1)}, bf16[3,4,512]{2,1,0:T(4,128)(2,1)S(1)}) custom-call(s32[4]{0:T(128)} %refs_0_.1, s32[4]{0:T(128)} %refs_1_.1, s32[4]{0:T(128)} %refs_2_.1, bf16[4,256,256]{2,1,0:T(8,128)(2,1)} %refs_3_.1, bf16[4,256,256]{2,1,0:T(8,128)(2,1)} %refs_4_.1, bf16[3,4,2048]{2,1,0:T(4,128)(2,1)} %refs_5_.1, ...), custom_call_target="tpu_custom_call" | custom-call | tf_op jit(solution)/shard_map/pallas_call | solution.py:560
  40.1 0.6 %copy.20 = bf16[3,4,2048]{2,1,0:T(4,128)(2,1)} copy(bf16[3,4,2048]{2,1,0:T(4,128)(2,1)S(1)} %get-tuple-element.4) | data formatting | bytes 98304
  40.7 0.6 %copy.21 = bf16[3,4,512]{2,1,0:T(4,128)(2,1)} copy(bf16[3,4,512]{2,1,0:T(4,128)(2,1)S(1)} %get-tuple-element.5) | data formatting | bytes 24576

commit v6 on v5

--- a/solution.py
+++ b/solution.py
@@ -379,7 +379,7 @@
         )
         picks.append(jnp.sum(jnp.where(own, product, 0.0), axis=0, keepdims=True))
     arrived(one_part_in, ONE, N_CTX - 1)
-    sel_out[0] = jnp.concatenate(picks + [jnp.zeros((5, 128), F32)], axis=0)
+    sel_out[0] = jnp.concatenate(picks + [jnp.zeros((1, 128), F32)], axis=0)
     sel_in[me] = sel_out[0]
     over_sel(lambda device: send(sel_out.at[0], sel_in.at[me], SELECT, device))
 
@@ -443,7 +443,7 @@
     total = sel_in[0]
     for k in range(1, N_SEL):
         total += sel_in[k]
-    columns = jnp.transpose(total)
+    columns = jnp.transpose(jnp.concatenate([total, jnp.zeros((4, 128), F32)], axis=0))
     for s in range(SLOTS):
         hidden = state_ref[s]
         for t in range(3):
@@ -463,7 +463,7 @@
         mam_out[p] = returned(mam_rows, p)
         send(mam_out.at[p], mam_in.at[d], MAMBA, {"dp": p})
 
-    first_started(d, N_DP, mam_one)
+    over_dp(mam_one)
     mam_in[d] = returned(mam_rows, d)
 
     def picked(ref, i):
@@ -588,8 +588,8 @@
             pltpu.VMEM((N_CTX * 16, 128), F32),
             pltpu.VMEM((N_CTX * 16, 128), F32),
             pltpu.VMEM((3, 8, CHAN), F32),
-            pltpu.VMEM((1, 8, 128), F32),
-            pltpu.VMEM((N_SEL, 8, 128), F32),
+            pltpu.VMEM((1, 4, 128), F32),
+            pltpu.VMEM((N_SEL, 4, 128), F32),
             pltpu.VMEM((N_CTX, 16, 128), BF16),
             pltpu.VMEM((N_CTX, 16, 128), BF16),
             pltpu.VMEM((N_CTX, 32, 128), BF16),

time: 41.5 us -> 41.2 us (level)
  no operation moved by 1% of the time
where the time goes in v6:
time: 41.2 us; the launch traced here: 41 us
  Pallas kernels  39.2 us (95%)
  local copies, waits for them, and re-layouts  1.22 us (3%)
  between operations  0.65 us (2%)
    pallas_call x1, Pallas kernels, on_device(): pl.pallas_call(kernel, out_shape=(jax.ShapeDtypeStruct((3, SLOTS, 2048),...  39.2 us
    unnamed x2, local copies, waits for them, and re-layouts  1.22 us

profile of v6, /device:TPU:1, one launch (start us, length us, event | category | flops | bytes accessed | tf_op | source)
XLA Modules:
  0.0 41.0 jit_solution(17319966868570810274)
XLA Ops:
  0.6 39.2 %shard_map.167 = (bf16[3,4,2048]{2,1,0:T(4,128)(2,1)S(1)}, bf16[3,4,512]{2,1,0:T(4,128)(2,1)S(1)}) custom-call(s32[4]{0:T(128)} %refs_0_.1, s32[4]{0:T(128)} %refs_1_.1, s32[4]{0:T(128)} %refs_2_.1, bf16[4,256,256]{2,1,0:T(8,128)(2,1)} %refs_3_.1, bf16[4,256,256]{2,1,0:T(8,128)(2,1)} %refs_4_.1, bf16[3,4,2048]{2,1,0:T(4,128)(2,1)} %refs_5_.1, ...), custom_call_target="tpu_custom_call" | custom-call | tf_op jit(solution)/shard_map/pallas_call | solution.py:560
  39.8 0.6 %copy.20 = bf16[3,4,2048]{2,1,0:T(4,128)(2,1)} copy(bf16[3,4,2048]{2,1,0:T(4,128)(2,1)S(1)} %get-tuple-element.4) | data formatting | bytes 98304
  40.4 0.6 %copy.21 = bf16[3,4,512]{2,1,0:T(4,128)(2,1)} copy(bf16[3,4,512]{2,1,0:T(4,128)(2,1)S(1)} %get-tuple-element.5) | data formatting | bytes 24576

commit v7 on v6

--- a/solution.py
+++ b/solution.py
@@ -423,14 +423,16 @@
     first_value = pair_rows(fresh_one, 1)
     arrived(part_in, PART, N_CTX - 1)
     done, overall, denominator = finish(part_in, 16, first_score, first_value)
-    weight_log = jnp.broadcast_to(overall + jnp.log(denominator), (16, 128))
+    place = lax.broadcasted_iota(jnp.int32, (16, 128), 1) == lax.broadcasted_iota(jnp.int32, (16, 128), 0) % 4
+    weight_log = jnp.where(place, overall + jnp.log(denominator), 0.0)
     for s in range(SLOTS):
         back_rows[s * 8 : s * 8 + 4, :] = done[s * 4 : s * 4 + 4, :]
-        back_rows[s * 8 + 4 : s * 8 + 8, :] = weight_log[s * 4 : s * 4 + 4, :]
+        logs = jnp.sum(weight_log[s * 4 : s * 4 + 4, :], axis=0, keepdims=True)
+        back_rows[s * 8 + 4 : s * 8 + 8, :] = jnp.broadcast_to(logs, (4, 128))
 
     def ans_one(p):
         ans_out[p] = returned(back_rows, p)
-        send(ans_out.at[p], ans_in.at[d], ANSWER, {"dp": p})
+        send(ans_out.at[p, pl.ds(0, 5)], ans_in.at[d, pl.ds(0, 5)], ANSWER, {"dp": p})
 
     first_started(d, N_DP, ans_one)
     ans_in[d] = returned(back_rows, d)
@@ -466,16 +468,17 @@
     over_dp(mam_one)
     mam_in[d] = returned(mam_rows, d)
 
-    def picked(ref, i):
-        total = ref[0] * member[i, 0:1, :]
+    def picked(ref, i, rows=8):
+        total = ref[0, 0:rows, :] * member[i, 0:1, :]
         for g in range(1, N_DP):
-            total += ref[g] * member[i, g : g + 1, :]
+            total += ref[g, 0:rows, :] * member[i, g : g + 1, :]
         return total
 
-    arrived(ans_in, ANSWER, N_DP - 1)
-    found = [picked(ans_in, i) for i in range(SLOTS)]
+    arrived(ans_in.at[:, pl.ds(0, 5)], ANSWER, N_DP - 1)
+    found = [picked(ans_in, i, 5) for i in range(SLOTS)]
     cached = jnp.concatenate([x[0:4, :] for x in found], axis=0)
-    cached_log = jnp.concatenate([x[4:8, :] for x in found], axis=0)[:, 0:1]
+    logs = jnp.concatenate([jnp.broadcast_to(x[4:5, :], (4, 128)) for x in found], axis=0)
+    cached_log = jnp.sum(jnp.where(place, logs, 0.0), axis=1, keepdims=True)
     overall = jnp.maximum(cached_log, jnp.maximum(second_score, third_score))
     keeps = [jnp.exp(cached_log - overall), jnp.exp(second_score - overall)]
     keeps.append(jnp.where(last_step, jnp.exp(third_score - overall), 0.0))
@@ -504,7 +507,7 @@
     sent(one_part_out, ONE, N_CTX - 1)
     sent(sel_in, SELECT, N_SEL - 1)
     sent(part_out, PART, N_CTX - 1)
-    sent(ans_out, ANSWER, N_DP - 1)
+    sent(ans_out.at[:, pl.ds(0, 5)], ANSWER, N_DP - 1)
     sent(one_in, ONE_DONE, N_CTX - 1)
     sent(mam_out, MAMBA, N_DP - 1)
 

time: 41.2 us -> 41.2 us (level)
  no operation moved by 1% of the time
where the time goes in v7:
time: 41.2 us; the launch traced here: 41 us
  Pallas kernels  39.2 us (95%)
  local copies, waits for them, and re-layouts  1.22 us (3%)
  between operations  0.65 us (2%)
    pallas_call x1, Pallas kernels, on_device(): pl.pallas_call(kernel, out_shape=(jax.ShapeDtypeStruct((3, SLOTS, 2048),...  39.2 us
    unnamed x2, local copies, waits for them, and re-layouts  1.22 us

profile of v7, /device:TPU:1, one launch (start us, length us, event | category | flops | bytes accessed | tf_op | source)
XLA Modules:
  0.0 41.0 jit_solution(10809943910296013964)
XLA Ops:
  0.6 39.2 %shard_map.167 = (bf16[3,4,2048]{2,1,0:T(4,128)(2,1)S(1)}, bf16[3,4,512]{2,1,0:T(4,128)(2,1)S(1)}) custom-call(s32[4]{0:T(128)} %refs_0_.1, s32[4]{0:T(128)} %refs_1_.1, s32[4]{0:T(128)} %refs_2_.1, bf16[4,256,256]{2,1,0:T(8,128)(2,1)} %refs_3_.1, bf16[4,256,256]{2,1,0:T(8,128)(2,1)} %refs_4_.1, bf16[3,4,2048]{2,1,0:T(4,128)(2,1)} %refs_5_.1, ...), custom_call_target="tpu_custom_call" | custom-call | tf_op jit(solution)/shard_map/pallas_call | solution.py:563
  39.8 0.6 %copy.20 = bf16[3,4,2048]{2,1,0:T(4,128)(2,1)} copy(bf16[3,4,2048]{2,1,0:T(4,128)(2,1)S(1)} %get-tuple-element.4) | data formatting | bytes 98304
  40.4 0.6 %copy.21 = bf16[3,4,512]{2,1,0:T(4,128)(2,1)} copy(bf16[3,4,512]{2,1,0:T(4,128)(2,1)S(1)} %get-tuple-element.5) | data formatting | bytes 24576
